TPU v7x, 256 devices: a whole 4x4x8 slice. The times are simulated.
256 devices in a mesh: blk: 16 (over y_lo, x, core), grp: 16 (over z, y_hi).
Axes of the slice: x: 4, y: 4 (y_hi: 2, y_lo: 2; y = y_hi * 2 + y_lo), z: 8, core: 2. Of those that a mesh axis runs over, the one named last changes fastest.
Arguments:
- user_factors: bfloat16 [16, 32768, 256], P('grp', 'blk')
- item_factors: bfloat16 [2048, 256], P('blk'), may hold values from -1.5 to 1.5
- tile_user: int32 [16, 16, 8], P('blk', 'grp'), may hold values from 0 to 255, as said below
- tile_weight: bfloat16 [16, 16, 8, 128, 128], P('blk', 'grp'), may hold values from 0.024 to 40.5
- tile_target: bfloat16 [16, 16, 8, 128, 128], P('blk', 'grp'), may hold values from -16 to 16
Outputs:
- new_block: float32 [2048, 128], P(('blk', 'grp'))
Inputs may be any that keep to these rules, and one draw needn't show every extreme that they name: `tile_user`: for each item block and user group, 8 different user tiles in increasing order.
All inputs are finite; a program needn't handle non-finite values.
Results may differ from a plain program's by a relative error of at most 0.002.
The roundings to bfloat16 on the way count: a program that leaves them out, or rounds other values in their place, can miss the bound.
Values may be sent and summed in bfloat16 or wider, within the bound.
A program may use at most 128 MiB of HBM per device.

v0:
```python
import jax
import jax.numpy as jnp
from jax import lax
from jax.sharding import PartitionSpec as P

K = 256
KB = 128
TILE = 128
NT = 8


prior_weight = 0.05
item_group = 8


def weighted_hessian(cols, w_block, width):
    weighted = (
        cols.astype(jnp.float32)[:, :, None] * w_block.astype(jnp.float32)[:, None, :]
    ).astype(jnp.bfloat16)
    weighted = weighted.reshape(-1, width * KB)
    return jnp.einsum("ux,us->xs", weighted, w_block, preferred_element_type=jnp.float32)


def local(user_factors, item_factors, tile_user, tile_weight, tile_target):
    own_rows = user_factors[0]
    users_idx = tile_user[0, 0]
    weight = tile_weight[0, 0]
    target = tile_target[0, 0]
    groups = lax.axis_size("grp")
    share = TILE // groups
    offsets = jnp.arange(TILE, dtype=jnp.int32)
    group_gram = jnp.zeros((KB, K), jnp.float32)
    start_buffer = jnp.zeros((NT, TILE, K), jnp.bfloat16)
    piece = lax.all_gather(own_rows, "blk", axis=0, tiled=True)
    buffer = start_buffer
    partial_gram = group_gram
    entry_count = piece.shape[0]
    wanted = users_idx[:, None] * TILE + offsets[None, :]
    inside = (wanted >= 0) & (wanted < entry_count)
    picked = jnp.take(piece, jnp.clip(wanted, 0, entry_count - 1).reshape(-1), axis=0).reshape(
        NT, TILE, K
    )
    buffer = jnp.where(inside[:, :, None], picked, buffer)
    buffer, group_gram = (buffer, partial_gram)
    local_gram = jnp.einsum(
        "us,ut->st", own_rows[:, :KB], own_rows, preferred_element_type=jnp.float32
    )
    gram = lax.psum(local_gram, ("blk", "grp"))
    rows_flat = buffer.reshape(-1, K)
    w_block = rows_flat[:, :KB]
    pred = jnp.einsum("uk,ik->ui", rows_flat, item_factors, preferred_element_type=jnp.float32)
    w_flat = weight.reshape(-1, TILE)
    resid = (
        w_flat.astype(jnp.float32) * (pred - target.reshape(-1, TILE).astype(jnp.float32))
    ).astype(jnp.bfloat16)
    h_mine = lax.dynamic_slice_in_dim(item_factors, lax.axis_index("grp") * share, share, 0)
    grad_part = jnp.einsum("ui,us->is", resid, w_block, preferred_element_type=jnp.float32)

    def hess_block(j):
        cols = lax.dynamic_slice_in_dim(w_flat, j * item_group, item_group, 1)
        return weighted_hessian(cols, w_block, item_group).reshape(item_group, KB, KB)

    hess_part = lax.map(hess_block, jnp.arange(TILE // item_group, dtype=jnp.int32)).reshape(
        TILE, KB, KB
    )
    hess, grad = (
        lax.psum_scatter(hess_part, "grp", scatter_dimension=0, tiled=True),
        lax.psum_scatter(grad_part, "grp", scatter_dimension=0, tiled=True),
    )
    hess = hess + prior_weight * gram[:, :KB][None]
    grad = grad + prior_weight * jnp.dot(
        h_mine.astype(jnp.float32), gram.T, precision=lax.Precision.HIGHEST
    )
    factor = jnp.linalg.cholesky(hess)
    delta = jax.scipy.linalg.cho_solve((factor, True), grad[..., None])[..., 0]
    return h_mine[:, :KB].astype(jnp.float32) - delta


def solution(mesh):
    return jax.shard_map(
        local,
        mesh=mesh,
        in_specs=(
            P("grp", "blk", None),
            P("blk", None),
            P("blk", "grp", None),
            P("blk", "grp", None, None, None),
            P("blk", "grp", None, None, None),
        ),
        out_specs=P(("blk", "grp"), None),
        check_vma=False,
    )
```

profile of v0, /device:TPU:32, one launch (start us, length us, event | category | flops | bytes accessed | tf_op | source)
XLA Modules:
  0.0 854.1 jit_solution(9507834067453046272)
XLA Ops:
  8.1 2.4 fusion.16
  11.5 1.1 copy.19
  12.6 94.5 %all-gather.3.cloned.1.call-done = bf16[1,32768,256]{2,1,0:T(8,128)(2,1)} async-done(((bf16[1,2048,256]{2,1,0:T(8,128)(2,1)}), bf16[1,32768,256]{2,1,0:T(8,128)(2,1)}) %all-gather.3.cloned.1.call-update) | async-done | bytes 16777232 | tf_op jit(solution)/shard_map/all_gather | solution.py:34
  107.2 11.4 %gather_fusion = bf16[1024,256]{1,0:T(8,128)(2,1)S(1)} fusion(bf16[32768,256]{1,0:T(8,128)(2,1)} %bitcast.75, s32[1024]{0:T(1024)S(1)} %broadcast_clamp_fusion), kind=kCustom, calls=%fused_computation | custom fusion | bytes 1052672 | tf_op jit(solution)/shard_map/jit(_take)/gather | solution.py:40
  118.9 1.2 fusion.14
  120.4 49.6 %while.10 = (s32[]{:T(128)}, f32[16,8,128,128]{2,3,1,0:T(8,128)}, s32[16]{0:T(128)S(1)}, bf16[1024,128]{0,1:T(8,128)(2,1)S(1)}, bf16[1024,128]{1,0:T(8,128)(2,1)...) while((s32[]{:T(128)}, f32[16,8,128,128]{2,3,1,0:T(8,128)}, s32[16]{0:T(128)S(1)}, ...), condition=%wide.region_1.2_spmd, body=%wide.region_0.1_spmd.sunk | while | flops 270540800 | bytes 2179239 | solution.py:63
  121.9 1.6 fusion.43
  125.0 1.6 fusion.43
  128.1 1.6 fusion.43
  131.2 1.6 fusion.43
  134.3 1.6 fusion.43
  137.4 1.6 fusion.43
  140.5 1.6 fusion.43
  143.6 1.6 fusion.43
  146.7 1.6 fusion.43
  149.7 1.7 fusion.43
  152.9 1.7 fusion.43
  156.0 1.6 fusion.43
  159.1 1.6 fusion.43
  162.2 1.6 fusion.43
  165.3 1.6 fusion.43
  168.4 1.7 fusion.43
  171.4 122.7 %all-reduce.4.cloned.1.call-done = f32[128,256]{1,0:T(8,128)} async-done(((f32[128,256]{1,0:T(8,128)}), f32[128,256]{1,0:T(8,128)}) %all-reduce.4.cloned.1.call-update) | async-done | bytes 131088 | tf_op jit(solution)/shard_map/psum | solution.py:48
  294.1 0.8 slice_multiply_fusion
  295.0 150.6 %all-reduce.6.cloned.1.call-done = f32[128,128]{1,0:T(8,128)} async-done(((f32[128,128]{1,0:T(8,128)}), f32[128,128]{1,0:T(8,128)}) %all-reduce.6.cloned.1.call-update) | async-done | bytes 65552
  445.7 1.1 fusion.15
  446.7 222.6 %reduce-scatter.2.cloned.1.call-done = f32[8,128,128]{1,2,0:T(8,128)} async-done(((f32[128,128,128]{1,2,0:T(8,128)}), f32[8,128,128]{1,2,0:T(8,128)}) %reduce-scatter.2.cloned.1.call-update) | async-done | bytes 524304 | tf_op jit(solution)/shard_map/reduce_scatter | solution.py:67
  669.3 1.1 broadcast_add_fusion
  670.6 1.1 fusion.22
  671.7 93.8 %custom-call.11 = f32[8,128,128]{2,1,0:T(8,128)S(1)} custom-call(f32[8,128,128]{2,1,0:T(8,128)S(1)} %fusion.22), custom_call_target="Cholesky" | custom-call | tf_op jit(solution)/shard_map/jit(cholesky)/cholesky | solution.py:74
  765.8 78.6 %custom-call.12 = f32[8,1,128,128]{2,3,1,0:T(8,128)S(1)} custom-call(f32[8,1,128,128]{3,2,1,0:T(8,128)S(1)} %select_bitcast_fusion), custom_call_target="InvertDiagBlocksLowerTriangular" | custom-call | tf_op jit(solution)/shard_map/jit(_cho_solve)/vmap()/triangular_solve | solution.py:75
  845.0 0.9 fusion.19
  (84 shorter events, 17.5 us)
Async XLA Ops:
  7.4 111.5 %copy-start = (bf16[1,1,8,128,128]{4,3,2,1,0:T(8,128)(2,1)S(1)}, bf16[1,1,8,128,128]{4,3,2,1,0:T(8,128)(2,1)}, u32[]{:S(2)}) copy-start(bf16[1,1,8,128,128]{4,3,2,1,0:T(8,128)(2,1)} %param.10) | copy-start | bytes 786436
  7.4 111.5 %copy-start.1 = (bf16[128,256]{1,0:T(8,128)(2,1)S(1)}, bf16[128,256]{1,0:T(8,128)(2,1)}, u32[]{:S(2)}) copy-start(bf16[128,256]{1,0:T(8,128)(2,1)} %param.8) | copy-start | bytes 196612
  7.4 111.5 %copy-start.2 = (bf16[1,1,8,128,128]{4,3,2,1,0:T(8,128)(2,1)S(1)}, bf16[1,1,8,128,128]{4,3,2,1,0:T(8,128)(2,1)}, u32[]{:S(2)}) copy-start(bf16[1,1,8,128,128]{4,3,2,1,0:T(8,128)(2,1)} %param.11) | copy-start | bytes 786436
  7.4 99.8 %all-gather.3.cloned.1.call-start = ((), (), s32[]{:S(2)}) async-start(), calls=%async_computation.3 | async-start | bytes 17825792 | tf_op jit(solution)/shard_map/all_gather | solution.py:34
  8.1 286.0 %all-reduce.4.cloned.1.call-start = ((), (), s32[]{:S(2)}) async-start(), calls=%async_computation.2 | async-start | bytes 262144 | tf_op jit(solution)/shard_map/psum | solution.py:48
  10.6 435.1 %all-reduce.6.cloned.1.call-start = ((), (), s32[]{:S(2)}) async-start(), calls=%async_computation.4 | async-start | bytes 131072
  120.2 549.1 %reduce-scatter.2.cloned.1.call-start = ((), (), s32[]{:S(2)}) async-start(), calls=%async_computation.1 | async-start | bytes 8912896 | tf_op jit(solution)/shard_map/reduce_scatter | solution.py:67
  120.4 49.6 %copy-start.3 = (u32[256]{0:T(256)S(1)}, u32[256]{0:T(256)}, u32[]{:S(2)}) copy-start(u32[256]{0:T(256)} %constant.105) | copy-start | bytes 3076
Sparse Core Ops, SparseCore 0:
  10.0 97.0 all-gather.2
Sparse Core Ops, SparseCore 1:
  14.1 279.9 all-reduce.3
  296.6 149.0 all-reduce.5
  450.2 219.1 reduce-scatter.1
where the time goes:
time: 856 us; the launch traced here: 854 us
  waiting for transfers between devices  591 us (69%)
  other arithmetic  178 us (21%)
  matrix products  32.4 us (4%)
  local copies, waits for them, and re-layouts  26 us (3%)
  between operations  15.8 us (2%)
  loops' own time  10.5 us (1%)
    reduce_scatter x1, waiting for transfers between devices, local(): lax.psum_scatter(hess_part, 'grp', scatter_dimension=0, tiled=True)  223 us
    unnamed x5, waiting for transfers between devices  151 us
    psum x1, waiting for transfers between devices, local(): gram = lax.psum(local_gram, ('blk', 'grp'))  123 us
    all_gather x1, waiting for transfers between devices, local(): piece = lax.all_gather(own_rows, 'blk', axis=0, tiled=True)  94.5 us
    another operation x4, other arithmetic, local(): factor = jnp.linalg.cholesky(hess)  94 us
    another operation x3, other arithmetic, local(): delta = jax.scipy.linalg.cho_solve((factor, True), grad[..., None])[..., 0]  78.7 us
    dot_general x16, matrix products, weighted_hessian(): jnp.einsum('ux,us->xs', weighted, w_block, preferred_element_type=jnp.flo...  26.2 us
  transfers between devices with their start and end apart: 4, of which 4 were waited for; matrix products, arithmetic and copies ran while one was open for 7% of the time, Pallas kernels for 0%

commit v1 on v0

v1 whole, which is shorter than its diff:
```python
import functools

import jax
import jax.numpy as jnp
from jax import lax
from jax.experimental import pallas as pl
from jax.experimental.pallas import tpu as pltpu
from jax.sharding import PartitionSpec as P

F32 = jnp.float32
BF16 = jnp.bfloat16
MESH = pl.DeviceIdType.MESH
K = 256
KB = 128
TILE = 128
NT = 8
PRIOR = 0.05
NI = 8
OWN = 16
ROWS = 64
NQ = TILE // ROWS
NCH = 2 * NQ
CU = NT * ROWS
NZ = 8
BOTH_LAST = (((1,), (1,)), ((), ()))
BOTH_FIRST = (((0,), (0,)), ((), ()))


def gather_kernel(
    user_ref, tile_ref, item_ref, weight_ref, target_ref,
    hess_ref, grad_ref, gram_ref,
    pools, far_a, far_b, out_p, out_m, in_a, in_b, in_p, in_m, rights, zbufs,
    reqs, item, weight, target, wt_own, tt_own, wz, hacc, hin, gsend, gin,
    gpart, gin1, gone, gin2, gtwo, gall, local_sem, send_sem, recv_sem,
):
    me_b, me_g = lax.axis_index("blk"), lax.axis_index("grp")
    y_lo, x, core = me_b // 8, lax.rem(me_b // 2, 4), lax.rem(me_b, 2)
    z, y_hi = me_g // 2, lax.rem(me_g, 2)
    own = y_lo * 2 + core
    across = (1 - y_lo) * 2 + core
    sibling = (me_b + 1 - 2 * core, me_g)
    y_peer = (lax.rem(me_b + 8, 16), me_g)
    x_at = [lax.rem(x + k, 4) for k in range(4)]
    x_peer = [(y_lo * 8 + x_at[k] * 2 + core, me_g) for k in range(4)]
    z_at = [lax.rem(z + k, NZ) for k in range(NZ)]
    z_peer = [(me_b, z_at[k] * 2 + y_hi) for k in range(NZ)]
    blk_at = [lax.rem(me_b + k, 16) for k in range(16)]
    grp_at = [lax.rem(me_g + k, 16) for k in range(16)]
    blk_peer = [(blk_at[k], me_g) for k in range(16)]
    grp_peer = [(me_b, grp_at[k]) for k in range(16)]
    partner = (me_b, me_g + 1 - 2 * y_hi)

    slots, sent = {}, []

    def slot(name):
        return slots.setdefault(name, len(slots))

    def send(name, src, dst, device):
        k = slot(name)
        copy = pltpu.make_async_remote_copy(
            src_ref=src, dst_ref=dst, send_sem=send_sem.at[k], recv_sem=recv_sem.at[k],
            device_id=device, device_id_type=MESH)
        copy.start()
        sent.append(copy)

    def arrived(name, dst):
        k = slot(name)
        pltpu.make_async_remote_copy(
            src_ref=dst, dst_ref=dst, send_sem=send_sem.at[k], recv_sem=recv_sem.at[k],
            device_id=sibling, device_id_type=MESH).wait_recv()

    locals_ = {}

    def fetch(name, src, dst):
        copy = pltpu.make_async_copy(src, dst, local_sem.at[len(locals_)])
        copy.start()
        locals_[name] = copy

    for c in range(NCH):
        rows, cols = (c % NQ) * ROWS, (c // NQ) * KB
        fetch(("pool", c), user_ref.at[:, pl.ds(rows, ROWS), pl.ds(cols, KB)], pools[c].at[own])
    fetch("tile", tile_ref, reqs.at[x])
    fetch("weight", weight_ref, weight)
    fetch("target", target_ref, target)
    fetch("item", item_ref, item)

    barrier = pltpu.get_barrier_semaphore()
    for k in range(1, 16):
        pl.semaphore_signal(barrier, inc=1, device_id=blk_peer[k], device_id_type=MESH)
        pl.semaphore_signal(barrier, inc=1, device_id=grp_peer[k], device_id_type=MESH)
    for copy in locals_.values():
        copy.wait()
    pl.semaphore_wait(barrier, 30)

    def send_chunk(c):
        send(("y", c), pools[c].at[own], pools[c].at[own], y_peer)
        send(("s", c), pools[c].at[own], pools[c].at[own], sibling)

    def forward_chunk(c):
        arrived(("y", c), pools[c].at[across])
        send(("f", c), pools[c].at[across], pools[c].at[across], sibling)

    def finish_pool(c):
        other = y_lo * 2 + 1 - core
        diagonal = (1 - y_lo) * 2 + 1 - core
        arrived(("s", c), pools[c].at[other])
        arrived(("f", c), pools[c].at[diagonal])

    def wanted(k, j):
        return reqs[x_at[k], 0, j]

    def column(t):
        return jnp.bitwise_and(jnp.right_shift(t, 5), 3)

    def pick(c, t):
        owner = jnp.right_shift(t, 7) * 2 + jnp.bitwise_and(jnp.right_shift(t, 4), 1)
        return pools[c][owner, jnp.bitwise_and(t, 15)]

    half = ROWS // 2

    def x_pack(c):
        for j in range(NT):
            v = pick(c, wanted(2, j))
            far_a[c][j] = v[:half]
            far_b[c][j] = v[half:]
        send(("xa", c), far_a[c], in_a[c], x_peer[1])
        send(("xb", c), far_b[c], in_b[c], x_peer[3])
        for j in range(NT):
            out_p[c][1, j] = pick(c, wanted(1, j))[half:]
            out_m[c][0, j] = pick(c, wanted(3, j))[:half]
        send(("p1", c), out_p[c].at[1], in_m[c].at[1], x_peer[1])
        send(("m0", c), out_m[c].at[0], in_p[c].at[0], x_peer[3])

    def x_merge(c):
        arrived(("xa", c), in_a[c])
        for j in range(NT):
            t = wanted(1, j)
            out_p[c][0, j] = jnp.where(column(t) == x, pick(c, t)[:half], in_a[c][j])
        send(("p0", c), out_p[c].at[0], in_m[c].at[0], x_peer[1])
        arrived(("xb", c), in_b[c])
        for j in range(NT):
            t = wanted(3, j)
            out_m[c][1, j] = jnp.where(column(t) == x, pick(c, t)[half:], in_b[c][j])
        send(("m1", c), out_m[c].at[1], in_p[c].at[1], x_peer[3])

    def x_final(c):
        arrived(("p1", c), in_m[c].at[1])
        arrived(("m0", c), in_p[c].at[0])
        arrived(("p0", c), in_m[c].at[0])
        arrived(("m1", c), in_p[c].at[1])
        for j in range(NT):
            t = wanted(0, j)
            away = jnp.bitwise_and(column(t) - x + 4, 3)
            mine = pick(c, t)
            first = jnp.where(away == 0, mine[:half], jnp.where(away == 1, in_p[c][0, j], in_m[c][0, j]))
            second = jnp.where(away == 0, mine[half:], jnp.where(away == 3, in_m[c][1, j], in_p[c][1, j]))
            if c < NQ:
                zbufs[c][z, j, :half] = first
                zbufs[c][z, j, half:] = second
            else:
                rights[c - NQ][j, :half] = first
                rights[c - NQ][j, half:] = second

    def z_start(q):
        send(("zr", q, 1), zbufs[q].at[z], zbufs[q].at[z], z_peer[1])
        send(("zl", q, 1), zbufs[q].at[z], zbufs[q].at[z], z_peer[7])

    def z_hop(q, h):
        if h < 4:
            from_left, from_right = z_at[NZ - h], z_at[h]
            arrived(("zr", q, h), zbufs[q].at[from_left])
            part = zbufs[q].at[from_left] if h < 3 else zbufs[q].at[from_left, pl.ds(0, NT // 2)]
            send(("zr", q, h + 1), part, part, z_peer[1])
            arrived(("zl", q, h), zbufs[q].at[from_right])
            part = zbufs[q].at[from_right] if h < 3 else zbufs[q].at[from_right, pl.ds(NT // 2, NT // 2)]
            send(("zl", q, h + 1), part, part, z_peer[7])
        else:
            arrived(("zr", q, 4), zbufs[q].at[z_at[4], pl.ds(0, NT // 2)])
            arrived(("zl", q, 4), zbufs[q].at[z_at[4], pl.ds(NT // 2, NT // 2)])

    def transposed(ref, out):
        span = TILE // ROWS
        for q in range(NQ):
            for p in range(NT // span):
                block = ref[p * span:(p + 1) * span, q * ROWS:(q + 1) * ROWS, :].reshape(TILE, TILE)
                out[:, :, pl.ds((q * (NT // span) + p) * TILE, TILE)] = block.T.reshape(NZ, 16, TILE)

    def send_weights():
        transposed(weight, wt_own)
        for k in range(1, NZ):
            send(("w", k), wt_own.at[z_at[k]], wz.at[z], z_peer[k])
        wz[z] = wt_own[z]

    def weights_arrived():
        for k in range(1, NZ):
            arrived(("w", k), wz.at[z_at[NZ - k]])

    def gram_start():
        left = jnp.zeros((KB, KB), F32)
        right = jnp.zeros((KB, KB), F32)
        for q in range(NQ):
            a = pools[q][own].reshape(OWN * ROWS, KB)
            b = pools[NQ + q][own].reshape(OWN * ROWS, KB)
            left += lax.dot_general(a, a, BOTH_FIRST, preferred_element_type=F32)
            right += lax.dot_general(a, b, BOTH_FIRST, preferred_element_type=F32)
        gpart[:, 0] = left.reshape(16, 8, KB)
        gpart[:, 1] = right.reshape(16, 8, KB)
        for k in range(1, 16):
            send(("g1", k), gpart.at[blk_at[k]], gin1.at[me_b], blk_peer[k])
        gin1[me_b] = gpart[me_b]

    def gram_second():
        for k in range(1, 16):
            arrived(("g1", k), gin1.at[blk_at[16 - k]])
        gone[...] = jnp.sum(gin1[...], axis=0)
        for k in range(1, 16):
            send(("g2", k), gone, gin2.at[me_g], grp_peer[k])
        gin2[me_g] = gone[...]

    def gram_third():
        for k in range(1, 16):
            arrived(("g2", k), gin2.at[grp_at[16 - k]])
        gtwo[...] = jnp.sum(gin2[...], axis=0)
        for k in range(1, 16):
            send(("g3", k), gtwo, gall.at[me_b], blk_peer[k])
        gall[me_b] = gtwo[...]

    def gram_last():
        for k in range(1, 16):
            arrived(("g3", k), gall.at[blk_at[16 - k]])
        gram_ref[...] = gall[...]

    GROUP = 4

    def hess_piece(q, source, first=0, count=16, start=False):
        users = zbufs[q][source].reshape(CU, KB)
        users_t = jnp.concatenate(
            [users[p * KB:(p + 1) * KB].T for p in range(CU // KB)], axis=1)
        users_t = users_t.reshape(KB // 16, 16, CU)
        scale = wz[source, :, pl.ds(q * CU, CU)].astype(F32)
        for i0 in range(0, 16, GROUP):
            lhs = []
            for i in range(i0, i0 + GROUP):
                row = jnp.broadcast_to(scale[i:i + 1], (16, CU)).astype(BF16)
                lhs.append((row[None] * users_t).reshape(KB, CU))
            part = jnp.dot(jnp.concatenate(lhs, axis=0), users, preferred_element_type=F32)
            part = part.reshape(GROUP, KB, KB)
            if start:
                hacc[i0:i0 + GROUP] = part
            else:
                hacc[i0:i0 + GROUP] += part

    def grad_start():
        total = jnp.zeros((TILE, KB), F32)
        items = item[...]
        for q in range(NQ):
            left = zbufs[q][z].reshape(CU, KB)
            right = rights[q][...].reshape(CU, KB)
            pred = lax.dot_general(items[:, :KB], left, BOTH_LAST, preferred_element_type=F32)
            pred += lax.dot_general(items[:, KB:], right, BOTH_LAST, preferred_element_type=F32)
            w = wt_own[:, :, pl.ds(q * CU, CU)].reshape(TILE, CU).astype(F32)
            t = tt_own[:, :, pl.ds(q * CU, CU)].reshape(TILE, CU).astype(F32)
            resid = (w * (pred - t)).astype(BF16)
            total += jnp.dot(resid, left, preferred_element_type=F32)
        gsend[...] = total.reshape(16, NI, KB)
        for k in range(1, 16):
            send(("gr", k), gsend.at[grp_at[k]], gin.at[me_g], grp_peer[k])
        gin[me_g] = gsend[me_g]

    def grad_last():
        for k in range(1, 16):
            arrived(("gr", k), gin.at[grp_at[16 - k]])
        grad_ref[...] = jnp.sum(gin[...], axis=0)

    def send_requests():
        for k in range(1, 4):
            send(("rq", k), reqs.at[x], reqs.at[x], x_peer[k])

    def requests_arrived():
        for k in range(1, 4):
            arrived(("rq", k), reqs.at[x_at[4 - k]])

    send_requests()
    send_chunk(0)
    send_weights()
    send_chunk(1)
    gram_start()
    transposed(target, tt_own)
    requests_arrived()
    forward_chunk(0)
    send_chunk(2)
    finish_pool(0)
    x_pack(0)
    x_merge(0)
    x_final(0)
    z_start(0)
    gram_second()
    forward_chunk(1)
    send_chunk(3)
    finish_pool(1)
    x_pack(1)
    weights_arrived()
    hess_piece(0, z, start=True)
    x_merge(1)
    z_hop(0, 1)
    x_final(1)
    z_start(1)
    hess_piece(0, z_at[7])
    forward_chunk(2)
    z_hop(0, 2)
    finish_pool(2)
    x_pack(2)
    hess_piece(0, z_at[1])
    x_merge(2)
    gram_third()
    z_hop(0, 3)
    z_hop(1, 1)
    forward_chunk(3)
    x_final(2)
    hess_piece(0, z_at[6])
    finish_pool(3)
    x_pack(3)
    hess_piece(0, z_at[2])
    hess_piece(0, z_at[5])
    x_merge(3)
    z_hop(1, 2)
    z_hop(0, 4)
    hess_piece(0, z_at[3])
    hess_piece(0, z_at[4])
    x_final(3)
    z_hop(1, 3)
    grad_start()
    hess_piece(1, z)
    for k in (7, 1, 6, 2, 5, 3):
        hess_piece(1, z_at[k])
    z_hop(1, 4)
    hess_piece(1, z_at[4])
    send("h", hacc.at[pl.ds((1 - y_hi) * NI, NI)], hin, partner)
    gram_last()
    grad_last()
    arrived("h", hin)
    hess_ref[...] = hacc[pl.ds(y_hi * NI, NI)] + hin[...]
    for copy in sent:
        copy.wait_send()
    assert len(slots) <= NSEM, len(slots)


NSEM = 160


def normal_equations(user_factors, item_factors, tile_user, tile_weight, tile_target):
    vm = pltpu.VMEM
    chunk = (NT, ROWS // 2, KB)
    both = (2,) + chunk
    return pl.pallas_call(
        gather_kernel,
        out_shape=(
            jax.ShapeDtypeStruct((NI, KB, KB), F32),
            jax.ShapeDtypeStruct((NI, KB), F32),
            jax.ShapeDtypeStruct((16, 2, 8, KB), F32),
        ),
        in_specs=[pl.BlockSpec(memory_space=pl.ANY)] * 5,
        out_specs=(pl.BlockSpec(memory_space=pltpu.VMEM),) * 3,
        scratch_shapes=[
            [vm((4, OWN, ROWS, KB), BF16)] * NCH,
            [vm(chunk, BF16)] * NCH,
            [vm(chunk, BF16)] * NCH,
            [vm(both, BF16)] * NCH,
            [vm(both, BF16)] * NCH,
            [vm(chunk, BF16)] * NCH,
            [vm(chunk, BF16)] * NCH,
            [vm(both, BF16)] * NCH,
            [vm(both, BF16)] * NCH,
            [vm((NT, ROWS, KB), BF16)] * NQ,
            [vm((NZ, NT, ROWS, KB), BF16)] * NQ,
            pltpu.SMEM((4, 1, NT), jnp.int32),
            vm((TILE, K), BF16),
            vm((NT, TILE, TILE), BF16),
            vm((NT, TILE, TILE), BF16),
            vm((NZ, 16, NT * TILE), BF16),
            vm((NZ, 16, NT * TILE), BF16),
            vm((NZ, 16, NT * TILE), BF16),
            vm((16, KB, KB), F32),
            vm((NI, KB, KB), F32),
            vm((16, NI, KB), F32),
            vm((16, NI, KB), F32),
            vm((16, 2, 8, KB), F32),
            vm((16, 2, 8, KB), F32),
            vm((2, 8, KB), F32),
            vm((16, 2, 8, KB), F32),
            vm((2, 8, KB), F32),
            vm((16, 2, 8, KB), F32),
            pltpu.SemaphoreType.DMA((NCH + 4,)),
            pltpu.SemaphoreType.DMA((NSEM,)),
            pltpu.SemaphoreType.DMA((NSEM,)),
        ],
        compiler_params=pltpu.CompilerParams(
            collective_id=0, has_side_effects=True, vmem_limit_bytes=48 * 1024 * 1024),
        name="normal_equations",
    )(user_factors, tile_user, item_factors, tile_weight, tile_target)


PANEL = 8
RB = 32


def lane_bcast(v, lane):
    return jnp.broadcast_to(v[:, lane:lane+1], v.shape)

def tree(xs):
    while len(xs) > 1:
        xs = [xs[i] + xs[i+1] if i+1 < len(xs) else xs[i] for i in range(0, len(xs), 2)]
    return xs[0]

def sweep_inverse(d, n):
    g = lambda i, j: d[(i, j) if i <= j else (j, i)]
    for k in range(n):
        inv = 1.0 / g(k, k)
        scaled = {i: g(i, k) * inv for i in range(n) if i != k}
        new = {}
        for i in range(n):
            for j in range(i, n):
                if i == k and j == k:
                    new[(i, j)] = -inv
                elif i == k:
                    new[(i, j)] = scaled[j]
                elif j == k:
                    new[(i, j)] = scaled[i]
                else:
                    new[(i, j)] = d[(i, j)] - scaled[i] * g(j, k)
        d = new
        g = lambda i, j, d=d: d[(i, j) if i <= j else (j, i)]
    return {ij: -v for ij, v in d.items()}

def solve_kernel(hess_ref, grad_ref, gram_ref, item_ref, out_ref, a_ref, dinv_ref):
    lane = lax.broadcasted_iota(jnp.int32, (NI, KB), 1)
    gram_s = gram_ref[:, 0].reshape(KB, KB)
    gram_r = gram_ref[:, 1].reshape(KB, KB)
    item = item_ref[...].astype(F32)
    dims = (((1,), (1,)), ((), ()))
    hi = lax.Precision.HIGHEST
    b = grad_ref[...] + PRIOR * (
        lax.dot_general(item[:, :KB], gram_s, dims, precision=hi, preferred_element_type=F32)
        + lax.dot_general(item[:, KB:], gram_r, dims, precision=hi, preferred_element_type=F32))
    for i in range(NI):
        h = hess_ref[i] + PRIOR * gram_s
        a_ref[pl.ds(i, KB, stride=NI), :] = 0.5 * (h + h.T)
    pairs = [(i, j) for i in range(PANEL) for j in range(i, PANEL)]
    for p in range(KB // PANEL):
        k0 = p * PANEL
        rows = [a_ref[pl.ds((k0 + j) * NI, NI), :] for j in range(PANEL)]
        dinv = sweep_inverse({(i, j): lane_bcast(rows[i], k0 + j) for i, j in pairs}, PANEL)
        for n, ij in enumerate(pairs):
            dinv_ref[p, n] = dinv[ij]
        if p + 1 == KB // PANEL:
            break
        kept = [jnp.where(lane >= k0 + PANEL, r, 0.0) for r in rows]
        ws = [tree([dinv[(min(i, j), max(i, j))] * kept[j] for j in range(PANEL)]) for i in range(PANEL)]
        b = b - tree([lane_bcast(b, k0 + j) * ws[j] for j in range(PANEL)])
        def update(base, count):
            vs = [a_ref[pl.ds(base + q * NI, NI), :] for q in range(count)]
            vs = [v - tree([lane_bcast(v, k0 + j) * ws[j] for j in range(PANEL)]) for v in vs]
            for q in range(count):
                a_ref[pl.ds(base + q * NI, NI), :] = vs[q]
        left = KB - k0 - PANEL
        if left % RB:
            update((k0 + PANEL) * NI, left % RB)
        if left // RB:
            first = (k0 + PANEL + left % RB) // RB
            @pl.loop(first, KB // RB)
            def _(g):
                update(pl.multiple_of(g * (RB * NI), RB * NI), RB)
    x = jnp.zeros((NI, KB), F32)
    for p in range(KB // PANEL - 1, -1, -1):
        k0 = p * PANEL
        bs = [lane_bcast(b, k0 + j) for j in range(PANEL)]
        dinv = {ij: dinv_ref[p, n] for n, ij in enumerate(pairs)}
        xs = [tree([dinv[(min(i, j), max(i, j))] * bs[j] for j in range(PANEL)]) for i in range(PANEL)]
        for j in range(PANEL):
            x = jnp.where(lane == k0 + j, xs[j], x)
        if p:
            b = b - tree([xs[j] * jnp.where(lane < k0, a_ref[pl.ds((k0 + j) * NI, NI), :], 0.0) for j in range(PANEL)])
    out_ref[...] = item[:, :KB] - x

def solve(hess, grad, gram, item):
    return pl.pallas_call(
        solve_kernel,
        out_shape=jax.ShapeDtypeStruct((NI, KB), F32),
        in_specs=[pl.BlockSpec(memory_space=pltpu.VMEM)]*4,
        out_specs=pl.BlockSpec(memory_space=pltpu.VMEM),
        scratch_shapes=[pltpu.VMEM((KB*NI, KB), F32), pltpu.VMEM((KB//PANEL, PANEL*(PANEL+1)//2, NI, KB), F32)],
        name="block_solve",
    )(hess, grad, gram, item)


def local(user_factors, item_factors, tile_user, tile_weight, tile_target):
    hess, grad, gram = normal_equations(
        user_factors.reshape(OWN, TILE, K), item_factors, tile_user[0], tile_weight[0, 0], tile_target[0, 0])
    mine = lax.dynamic_slice_in_dim(item_factors, lax.axis_index("grp") * NI, NI, 0)
    return solve(hess, grad, gram, mine)


def solution(mesh):
    return jax.shard_map(
        local,
        mesh=mesh,
        in_specs=(
            P("grp", "blk", None),
            P("blk", None),
            P("blk", "grp", None),
            P("blk", "grp", None, None, None),
            P("blk", "grp", None, None, None),
        ),
        out_specs=P(("blk", "grp"), None),
        check_vma=False,
    )
```

time: 856 us -> 109 us (0.13)
  the two profiles are of different devices: /device:TPU:32 before, /device:TPU:1 now
where the time goes in v1:
time: 109 us
  Pallas kernels  101 us (93%)
  local copies, waits for them, and re-layouts  7.29 us (7%)
    pallas_call x1, Pallas kernels, normal_equations(): pl.pallas_call(gather_kernel, out_shape=(jax.ShapeDtypeStruct((NI, KB, KB...  80.7 us
    pallas_call x1, Pallas kernels, solve(): pl.pallas_call(solve_kernel, out_shape=jax.ShapeDtypeStruct((NI, KB), F32...  20.5 us
    unnamed x16, local copies, waits for them, and re-layouts  6 us

profile of v1, /device:TPU:1, one launch (start us, length us, event | category | flops | bytes accessed | tf_op | source)
XLA Modules:
  0.0 108.6 jit_solution(10989905908379667826)
XLA Ops:
  0.0 0.0 copy-start.7
  0.0 1.3 %constant_dynamic-slice_fusion.item_ref = bf16[8,256]{1,0:T(8,128)(2,1)} fusion(bf16[128,256]{1,0:T(8,128)(2,1)} %item_ref.1, s32[]{:T(128)S(6)} %select_n.3), kind=kLoop, calls=%fused_computation | loop fusion | bytes 8196 | tf_op jit(solution)/shard_map/dynamic_slice | solution.py:499
  1.3 0.0 copy-done.7
  1.3 0.0 copy-start
  1.3 1.2 %copy-done = bf16[1,2048,256]{2,1,0:T(8,128)(2,1)S(1)} copy-done((bf16[1,2048,256]{2,1,0:T(8,128)(2,1)S(1)}, bf16[1,2048,256]{2,1,0:T(8,128)(2,1)}, u32[]{:S(2)}) %copy-start) | copy-done | bytes 1048600
  2.5 0.0 copy-start.2
  2.5 0.9 copy-done.2
  3.5 0.0 copy-start.3
  3.5 0.9 copy-done.3
  4.4 0.0 copy-start.5
  4.4 0.8 copy-done.5
  5.3 80.7 %normal_equations.1 = (f32[8,128,128]{2,1,0:T(8,128)S(1)}, f32[8,128]{1,0:T(8,128)S(1)}, f32[16,2,8,128]{3,2,1,0:T(8,128)S(1)}) custom-call(bf16[16,128,256]{2,1,0:T(8,128)(2,1)S(1)} %bitcast.4, s32[1,8]{1,0:T(1,128)S(1)} %bitcast.7, bf16[128,256]{1,0:T(8,128)(2,1)S(1)} %copy-done.5, bf16[8,128,128]{2,1,0:T(8,128)(2,1)S(1)} %bitcast.5, ...), custom_call_target="tpu_custom_call" | custom-call | tf_op jit(solution)/shard_map/normal_equations/pallas_call | solution.py:355
  86.0 0.0 copy-start.1
  86.0 0.8 copy-done.1
  86.8 0.0 copy-start.4
  86.8 0.7 copy-done.4
  87.5 0.0 copy-start.6
  87.5 0.6 copy-done.6
  88.0 20.5 %block_solve.1 = f32[8,128]{1,0:T(8,128)} custom-call(f32[8,128,128]{2,1,0:T(8,128)} %copy-done.1, f32[8,128]{1,0:T(8,128)} %copy-done.6, f32[16,2,8,128]{3,2,1,0:T(8,128)} %copy-done.4, bf16[8,256]{1,0:T(8,128)(2,1)} %constant_dynamic-slice_fusion.item_ref), custom_call_target="tpu_custom_call" | custom-call | tf_op jit(solution)/shard_map/block_solve/pallas_call | solution.py:486
Async XLA Ops:
  0.0 1.3 %copy-start.7 = (s32[1,1,8]{2,1,0:T(1,128)S(1)}, s32[1,1,8]{2,1,0:T(1,128)}, u32[]{:S(2)}) copy-start(s32[1,1,8]{2,1,0:T(1,128)} %param.7) | copy-start | bytes 100
  1.3 1.2 %copy-start = (bf16[1,2048,256]{2,1,0:T(8,128)(2,1)S(1)}, bf16[1,2048,256]{2,1,0:T(8,128)(2,1)}, u32[]{:S(2)}) copy-start(bf16[1,2048,256]{2,1,0:T(8,128)(2,1)} %param.5) | copy-start | bytes 3145732
  2.5 0.9 copy-start.2
  3.5 0.9 copy-start.3
  4.4 0.8 copy-start.5
  86.0 0.8 copy-start.1
  86.8 0.7 copy-start.4
  87.5 0.6 copy-start.6

commit v2 on v1

--- a/solution.py
+++ b/solution.py
@@ -17,7 +17,7 @@
 PRIOR = 0.05
 NI = 8
 OWN = 16
-ROWS = 64
+ROWS = 32
 NQ = TILE // ROWS
 NCH = 2 * NQ
 CU = NT * ROWS
@@ -28,9 +28,9 @@
 
 def gather_kernel(
     user_ref, tile_ref, item_ref, weight_ref, target_ref,
-    hess_ref, grad_ref, gram_ref,
+    system_ref, rhs_ref, mine_ref,
     pools, far_a, far_b, out_p, out_m, in_a, in_b, in_p, in_m, rights, zbufs,
-    reqs, item, weight, target, wt_own, tt_own, wz, hacc, hin, gsend, gin,
+    reqs, item, itemf, weight, target, wt_own, tt_own, wz, hacc, hsend, hin, hown, gsend, gin,
     gpart, gin1, gone, gin2, gtwo, gall, local_sem, send_sem, recv_sem,
 ):
     me_b, me_g = lax.axis_index("blk"), lax.axis_index("grp")
@@ -76,6 +76,10 @@
         copy.start()
         locals_[name] = copy
 
+    barrier = pltpu.get_barrier_semaphore()
+    for k in range(1, 16):
+        pl.semaphore_signal(barrier, inc=1, device_id=blk_peer[k], device_id_type=MESH)
+        pl.semaphore_signal(barrier, inc=1, device_id=grp_peer[k], device_id_type=MESH)
     for c in range(NCH):
         rows, cols = (c % NQ) * ROWS, (c // NQ) * KB
         fetch(("pool", c), user_ref.at[:, pl.ds(rows, ROWS), pl.ds(cols, KB)], pools[c].at[own])
@@ -84,12 +88,8 @@
     fetch("target", target_ref, target)
     fetch("item", item_ref, item)
 
-    barrier = pltpu.get_barrier_semaphore()
-    for k in range(1, 16):
-        pl.semaphore_signal(barrier, inc=1, device_id=blk_peer[k], device_id_type=MESH)
-        pl.semaphore_signal(barrier, inc=1, device_id=grp_peer[k], device_id_type=MESH)
-    for copy in locals_.values():
-        copy.wait()
+    for name in [("pool", c) for c in range(NCH)] + ["tile"]:
+        locals_[name].wait()
     pl.semaphore_wait(barrier, 30)
 
     def send_chunk(c):
@@ -186,6 +186,7 @@
                 out[:, :, pl.ds((q * (NT // span) + p) * TILE, TILE)] = block.T.reshape(NZ, 16, TILE)
 
     def send_weights():
+        locals_["weight"].wait()
         transposed(weight, wt_own)
         for k in range(1, NZ):
             send(("w", k), wt_own.at[z_at[k]], wz.at[z], z_peer[k])
@@ -228,27 +229,62 @@
     def gram_last():
         for k in range(1, 16):
             arrived(("g3", k), gall.at[blk_at[16 - k]])
-        gram_ref[...] = gall[...]
 
     GROUP = 4
 
-    def hess_piece(q, source, first=0, count=16, start=False):
-        users = zbufs[q][source].reshape(CU, KB)
+    def hess_piece(q, sources, start=False, last=False):
+        users = [zbufs[q][s].reshape(CU, KB) for s in sources]
         users_t = jnp.concatenate(
-            [users[p * KB:(p + 1) * KB].T for p in range(CU // KB)], axis=1)
-        users_t = users_t.reshape(KB // 16, 16, CU)
-        scale = wz[source, :, pl.ds(q * CU, CU)].astype(F32)
+            [u[p * KB:(p + 1) * KB].T for u in users for p in range(CU // KB)], axis=1)
+        width = CU * len(sources)
+        users_t = users_t.reshape(KB // 16, 16, width)
+        users = jnp.concatenate(users, axis=0)
+        scale = jnp.concatenate([wz[s, :, pl.ds(q * CU, CU)].astype(F32) for s in sources], axis=1)
+        theirs = jnp.where(y_hi == 0, scale[8:], scale[:8])
+        ours = jnp.where(y_hi == 0, scale[:8], scale[8:])
+        scale = jnp.concatenate([theirs, ours], axis=0)
         for i0 in range(0, 16, GROUP):
             lhs = []
             for i in range(i0, i0 + GROUP):
-                row = jnp.broadcast_to(scale[i:i + 1], (16, CU)).astype(BF16)
-                lhs.append((row[None] * users_t).reshape(KB, CU))
+                row = jnp.broadcast_to(scale[i:i + 1], (16, width)).astype(BF16)
+                lhs.append((row[None] * users_t).reshape(KB, width))
             part = jnp.dot(jnp.concatenate(lhs, axis=0), users, preferred_element_type=F32)
             part = part.reshape(GROUP, KB, KB)
             if start:
                 hacc[i0:i0 + GROUP] = part
             else:
                 hacc[i0:i0 + GROUP] += part
+            if last and i0 < NI:
+                for i in range(i0, i0 + GROUP, 2):
+                    fold(i)
+
+    def row_col():
+        return (lax.broadcasted_iota(jnp.int32, (KB, KB), 0), lax.broadcasted_iota(jnp.int32, (KB, KB), 1))
+
+    def fold(i):
+        row, col = row_col()
+        hsend[i // 2, :KB] = jnp.where(row <= col, hacc[i], hacc[i + 1])
+        diag = jnp.sum(jnp.where(row == col, hacc[i + 1], 0.0), axis=0, keepdims=True)
+        hsend[i // 2, KB:] = jnp.broadcast_to(diag, (8, KB))
+        send(("h", i), hsend.at[i // 2], hin.at[i // 2], partner)
+
+    def own_systems():
+        prior = PRIOR * gall[:, 0].reshape(KB, KB)
+        for i in range(NI):
+            h = hacc[NI + i]
+            hown[i] = 0.5 * (h + h.T) + prior
+
+    def join_systems():
+        row, col = row_col()
+        for i in range(0, NI, 2):
+            arrived(("h", i), hin.at[i // 2])
+            square = hin[i // 2, :KB]
+            turned = square.T
+            diag = hin[i // 2, KB:KB + 1]
+            first = jnp.where(row <= col, square, turned)
+            second = jnp.where(row > col, square, jnp.where(row == col, diag, turned))
+            system_ref[pl.ds(i, KB, stride=NI), :] = hown[i] + first
+            system_ref[pl.ds(i + 1, KB, stride=NI), :] = hown[i + 1] + second
 
     def grad_start():
         total = jnp.zeros((TILE, KB), F32)
@@ -267,10 +303,26 @@
             send(("gr", k), gsend.at[grp_at[k]], gin.at[me_g], grp_peer[k])
         gin[me_g] = gsend[me_g]
 
+    def rhs_start():
+        itemf[...] = item[...].astype(F32)
+        mine = itemf[pl.ds(me_g * NI, NI), :]
+        mine_ref[...] = mine[:, :KB]
+        exact = lax.Precision.HIGHEST
+        rhs_ref[...] = PRIOR * (
+            lax.dot_general(mine[:, :KB], gall[:, 0].reshape(KB, KB), BOTH_LAST,
+                            precision=exact, preferred_element_type=F32)
+            + lax.dot_general(mine[:, KB:], gall[:, 1].reshape(KB, KB), BOTH_LAST,
+                              precision=exact, preferred_element_type=F32))
+
     def grad_last():
         for k in range(1, 16):
             arrived(("gr", k), gin.at[grp_at[16 - k]])
-        grad_ref[...] = jnp.sum(gin[...], axis=0)
+        rhs_ref[...] += jnp.sum(gin[...], axis=0)
+
+    def target_ready():
+        locals_["target"].wait()
+        transposed(target, tt_own)
+        locals_["item"].wait()
 
     def send_requests():
         for k in range(1, 4):
@@ -282,70 +334,108 @@
 
     send_requests()
     send_chunk(0)
+    send_chunk(1)
+    send_chunk(2)
     send_weights()
-    send_chunk(1)
     gram_start()
-    transposed(target, tt_own)
+    target_ready()
     requests_arrived()
     forward_chunk(0)
-    send_chunk(2)
+    send_chunk(3)
     finish_pool(0)
     x_pack(0)
+    gram_second()
+    forward_chunk(1)
+    send_chunk(4)
     x_merge(0)
+    finish_pool(1)
+    x_pack(1)
+    forward_chunk(2)
+    send_chunk(5)
     x_final(0)
     z_start(0)
-    gram_second()
-    forward_chunk(1)
-    send_chunk(3)
-    finish_pool(1)
-    x_pack(1)
     weights_arrived()
-    hess_piece(0, z, start=True)
     x_merge(1)
+    finish_pool(2)
+    x_pack(2)
+    gram_third()
+    forward_chunk(3)
+    send_chunk(6)
     z_hop(0, 1)
     x_final(1)
     z_start(1)
-    hess_piece(0, z_at[7])
-    forward_chunk(2)
-    z_hop(0, 2)
-    finish_pool(2)
-    x_pack(2)
-    hess_piece(0, z_at[1])
     x_merge(2)
-    gram_third()
-    z_hop(0, 3)
-    z_hop(1, 1)
-    forward_chunk(3)
-    x_final(2)
-    hess_piece(0, z_at[6])
+    hess_piece(0, (z_at[7], z_at[1]), start=True)
     finish_pool(3)
     x_pack(3)
-    hess_piece(0, z_at[2])
-    hess_piece(0, z_at[5])
+    forward_chunk(4)
+    send_chunk(7)
+    z_hop(0, 2)
+    z_hop(1, 1)
+    x_final(2)
+    z_start(2)
+    hess_piece(0, (z_at[6], z_at[2]))
     x_merge(3)
+    hess_piece(1, (z_at[7], z_at[1]))
+    finish_pool(4)
+    x_pack(4)
+    forward_chunk(5)
+    z_hop(0, 3)
     z_hop(1, 2)
+    z_hop(2, 1)
+    hess_piece(0, (z_at[5], z_at[3]))
+    x_final(3)
+    z_start(3)
+    hess_piece(1, (z_at[6], z_at[2]))
+    x_merge(4)
+    hess_piece(2, (z_at[7], z_at[1]))
+    finish_pool(5)
+    x_pack(5)
+    gram_last()
+    rhs_start()
+    forward_chunk(6)
     z_hop(0, 4)
-    hess_piece(0, z_at[3])
-    hess_piece(0, z_at[4])
-    x_final(3)
     z_hop(1, 3)
+    z_hop(2, 2)
+    hess_piece(0, (z, z_at[4]))
+    z_hop(3, 1)
+    hess_piece(1, (z_at[5], z_at[3]))
+    x_final(4)
+    hess_piece(2, (z_at[6], z_at[2]))
+    x_merge(5)
+    hess_piece(3, (z_at[7], z_at[1]))
+    finish_pool(6)
+    x_pack(6)
+    forward_chunk(7)
+    z_hop(1, 4)
+    z_hop(2, 3)
+    z_hop(3, 2)
+    hess_piece(1, (z, z_at[4]))
+    hess_piece(2, (z_at[5], z_at[3]))
+    x_final(5)
+    hess_piece(3, (z_at[6], z_at[2]))
+    x_merge(6)
+    finish_pool(7)
+    x_pack(7)
+    z_hop(2, 4)
+    z_hop(3, 3)
+    hess_piece(2, (z, z_at[4]))
+    hess_piece(3, (z_at[5], z_at[3]))
+    x_final(6)
+    x_merge(7)
+    z_hop(3, 4)
+    hess_piece(3, (z, z_at[4]), last=True)
+    x_final(7)
     grad_start()
-    hess_piece(1, z)
-    for k in (7, 1, 6, 2, 5, 3):
-        hess_piece(1, z_at[k])
-    z_hop(1, 4)
-    hess_piece(1, z_at[4])
-    send("h", hacc.at[pl.ds((1 - y_hi) * NI, NI)], hin, partner)
-    gram_last()
+    own_systems()
     grad_last()
-    arrived("h", hin)
-    hess_ref[...] = hacc[pl.ds(y_hi * NI, NI)] + hin[...]
+    join_systems()
     for copy in sent:
         copy.wait_send()
     assert len(slots) <= NSEM, len(slots)
 
 
-NSEM = 160
+NSEM = 260
 
 
 def normal_equations(user_factors, item_factors, tile_user, tile_weight, tile_target):
@@ -355,9 +445,9 @@
     return pl.pallas_call(
         gather_kernel,
         out_shape=(
-            jax.ShapeDtypeStruct((NI, KB, KB), F32),
+            jax.ShapeDtypeStruct((KB * NI, KB), F32),
             jax.ShapeDtypeStruct((NI, KB), F32),
-            jax.ShapeDtypeStruct((16, 2, 8, KB), F32),
+            jax.ShapeDtypeStruct((NI, KB), F32),
         ),
         in_specs=[pl.BlockSpec(memory_space=pl.ANY)] * 5,
         out_specs=(pl.BlockSpec(memory_space=pltpu.VMEM),) * 3,
@@ -375,12 +465,15 @@
             [vm((NZ, NT, ROWS, KB), BF16)] * NQ,
             pltpu.SMEM((4, 1, NT), jnp.int32),
             vm((TILE, K), BF16),
+            vm((TILE, K), F32),
             vm((NT, TILE, TILE), BF16),
             vm((NT, TILE, TILE), BF16),
             vm((NZ, 16, NT * TILE), BF16),
             vm((NZ, 16, NT * TILE), BF16),
             vm((NZ, 16, NT * TILE), BF16),
             vm((16, KB, KB), F32),
+            vm((NI // 2, KB + 8, KB), F32),
+            vm((NI // 2, KB + 8, KB), F32),
             vm((NI, KB, KB), F32),
             vm((16, NI, KB), F32),
             vm((16, NI, KB), F32),
@@ -395,7 +488,7 @@
             pltpu.SemaphoreType.DMA((NSEM,)),
         ],
         compiler_params=pltpu.CompilerParams(
-            collective_id=0, has_side_effects=True, vmem_limit_bytes=48 * 1024 * 1024),
+            collective_id=0, has_side_effects=True, vmem_limit_bytes=60 * 1024 * 1024),
         name="normal_equations",
     )(user_factors, tile_user, item_factors, tile_weight, tile_target)
 
@@ -432,19 +525,12 @@
         g = lambda i, j, d=d: d[(i, j) if i <= j else (j, i)]
     return {ij: -v for ij, v in d.items()}
 
-def solve_kernel(hess_ref, grad_ref, gram_ref, item_ref, out_ref, a_ref, dinv_ref):
+def solve_kernel(system_ref, rhs_ref, mine_ref, out_ref, a_ref, dinv_ref, sem):
+    load = pltpu.make_async_copy(system_ref, a_ref, sem)
+    load.start()
     lane = lax.broadcasted_iota(jnp.int32, (NI, KB), 1)
-    gram_s = gram_ref[:, 0].reshape(KB, KB)
-    gram_r = gram_ref[:, 1].reshape(KB, KB)
-    item = item_ref[...].astype(F32)
-    dims = (((1,), (1,)), ((), ()))
-    hi = lax.Precision.HIGHEST
-    b = grad_ref[...] + PRIOR * (
-        lax.dot_general(item[:, :KB], gram_s, dims, precision=hi, preferred_element_type=F32)
-        + lax.dot_general(item[:, KB:], gram_r, dims, precision=hi, preferred_element_type=F32))
-    for i in range(NI):
-        h = hess_ref[i] + PRIOR * gram_s
-        a_ref[pl.ds(i, KB, stride=NI), :] = 0.5 * (h + h.T)
+    b = rhs_ref[...]
+    load.wait()
     pairs = [(i, j) for i in range(PANEL) for j in range(i, PANEL)]
     for p in range(KB // PANEL):
         k0 = p * PANEL
@@ -480,24 +566,28 @@
             x = jnp.where(lane == k0 + j, xs[j], x)
         if p:
             b = b - tree([xs[j] * jnp.where(lane < k0, a_ref[pl.ds((k0 + j) * NI, NI), :], 0.0) for j in range(PANEL)])
-    out_ref[...] = item[:, :KB] - x
-
-def solve(hess, grad, gram, item):
+    out_ref[...] = mine_ref[...] - x
+
+def solve(system, rhs, mine):
+    vmem = pl.BlockSpec(memory_space=pltpu.VMEM)
     return pl.pallas_call(
         solve_kernel,
         out_shape=jax.ShapeDtypeStruct((NI, KB), F32),
-        in_specs=[pl.BlockSpec(memory_space=pltpu.VMEM)]*4,
-        out_specs=pl.BlockSpec(memory_space=pltpu.VMEM),
-        scratch_shapes=[pltpu.VMEM((KB*NI, KB), F32), pltpu.VMEM((KB//PANEL, PANEL*(PANEL+1)//2, NI, KB), F32)],
+        in_specs=[pl.BlockSpec(memory_space=pl.ANY), vmem, vmem],
+        out_specs=vmem,
+        scratch_shapes=[
+            pltpu.VMEM((KB * NI, KB), F32),
+            pltpu.VMEM((KB // PANEL, PANEL * (PANEL + 1) // 2, NI, KB), F32),
+            pltpu.SemaphoreType.DMA,
+        ],
+        compiler_params=pltpu.CompilerParams(vmem_limit_bytes=60 * 1024 * 1024),
         name="block_solve",
-    )(hess, grad, gram, item)
+    )(system, rhs, mine)
 
 
 def local(user_factors, item_factors, tile_user, tile_weight, tile_target):
-    hess, grad, gram = normal_equations(
-        user_factors.reshape(OWN, TILE, K), item_factors, tile_user[0], tile_weight[0, 0], tile_target[0, 0])
-    mine = lax.dynamic_slice_in_dim(item_factors, lax.axis_index("grp") * NI, NI, 0)
-    return solve(hess, grad, gram, mine)
+    return solve(*normal_equations(
+        user_factors.reshape(OWN, TILE, K), item_factors, tile_user[0], tile_weight[0, 0], tile_target[0, 0]))
 
 
 def solution(mesh):

time: 109 us -> 93.5 us (0.86)
  the two profiles are of different devices: /device:TPU:1 before, /device:TPU:32 now
where the time goes in v2:
time: 93.5 us; the launch traced here: 92.5 us
  Pallas kernels  92.3 us (99%)
    pallas_call x1, Pallas kernels, normal_equations(): pl.pallas_call(gather_kernel, out_shape=(jax.ShapeDtypeStruct((KB * NI, K...  71.3 us
    pallas_call x1, Pallas kernels, solve(): pl.pallas_call(solve_kernel, out_shape=jax.ShapeDtypeStruct((NI, KB), F32...  21 us

profile of v2, /device:TPU:32, one launch (start us, length us, event | category | flops | bytes accessed | tf_op | source)
XLA Modules:
  0.0 92.5 jit_solution(6673226245788557579)
XLA Ops:
  0.0 71.3 %normal_equations.1 = (f32[1024,128]{1,0:T(8,128)}, f32[8,128]{1,0:T(8,128)}, f32[8,128]{1,0:T(8,128)}) custom-call(bf16[16,128,256]{2,1,0:T(8,128)(2,1)} %bitcast.4, s32[1,8]{1,0:T(1,128)} %bitcast.7, bf16[128,256]{1,0:T(8,128)(2,1)} %item_ref.1, bf16[8,128,128]{2,1,0:T(8,128)(2,1)} %bitcast.5, bf16[8,128,128]{2,1,0:T(8,128)(2,1)} %bitcast.6), custom_call_target="tpu_custom_call" | custom-call | tf_op jit(solution)/shard_map/normal_equations/pallas_call | solution.py:445
  71.3 21.0 %block_solve.1 = f32[8,128]{1,0:T(8,128)} custom-call(f32[1024,128]{1,0:T(8,128)} %get-tuple-element.8.system_ref, f32[8,128]{1,0:T(8,128)} %get-tuple-element.9.rhs_ref, f32[8,128]{1,0:T(8,128)} %get-tuple-element.10.mine_ref), custom_call_target="tpu_custom_call" | custom-call | tf_op jit(solution)/shard_map/block_solve/pallas_call | solution.py:573

commit v3 on v2

--- a/solution.py
+++ b/solution.py
@@ -154,12 +154,47 @@
             mine = pick(c, t)
             first = jnp.where(away == 0, mine[:half], jnp.where(away == 1, in_p[c][0, j], in_m[c][0, j]))
             second = jnp.where(away == 0, mine[half:], jnp.where(away == 3, in_m[c][1, j], in_p[c][1, j]))
-            if c < NQ:
-                zbufs[c][z, j, :half] = first
-                zbufs[c][z, j, half:] = second
-            else:
-                rights[c - NQ][j, :half] = first
-                rights[c - NQ][j, half:] = second
+            put(c, j, first, second)
+
+    def x_pack_direct(c):
+        for j in range(NT):
+            v = pick(c, wanted(2, j))
+            far_a[c][j] = v[:half]
+            far_b[c][j] = v[half:]
+        send(("xa", c), far_a[c], in_a[c], x_peer[2])
+        send(("xb", c), far_b[c], in_b[c], x_peer[2])
+        for j in range(NT):
+            v = pick(c, wanted(1, j))
+            out_p[c][0, j] = v[:half]
+            out_p[c][1, j] = v[half:]
+            v = pick(c, wanted(3, j))
+            out_m[c][0, j] = v[:half]
+            out_m[c][1, j] = v[half:]
+        send(("p0", c), out_p[c], in_m[c], x_peer[1])
+        send(("m0", c), out_m[c], in_p[c], x_peer[3])
+
+    def x_final_direct(c):
+        arrived(("p0", c), in_m[c])
+        arrived(("m0", c), in_p[c])
+        arrived(("xa", c), in_a[c])
+        arrived(("xb", c), in_b[c])
+        for j in range(NT):
+            t = wanted(0, j)
+            away = jnp.bitwise_and(column(t) - x + 4, 3)
+            mine = pick(c, t)
+            parts = []
+            for p, far in ((0, in_a[c][j]), (1, in_b[c][j])):
+                near = jnp.where(away == 1, in_p[c][p, j], in_m[c][p, j])
+                parts.append(jnp.where(away == 0, mine[p * half:(p + 1) * half], jnp.where(away == 2, far, near)))
+            put(c, j, *parts)
+
+    def put(c, j, first, second):
+        if c < NQ:
+            zbufs[c][z, j, :half] = first
+            zbufs[c][z, j, half:] = second
+        else:
+            rights[c - NQ][j, :half] = first
+            rights[c - NQ][j, half:] = second
 
     def z_start(q):
         send(("zr", q, 1), zbufs[q].at[z], zbufs[q].at[z], z_peer[1])
@@ -339,94 +374,90 @@
     send_weights()
     gram_start()
     target_ready()
-    requests_arrived()
     forward_chunk(0)
     send_chunk(3)
+    requests_arrived()
     finish_pool(0)
-    x_pack(0)
-    gram_second()
+    x_pack_direct(0)
     forward_chunk(1)
     send_chunk(4)
-    x_merge(0)
+    weights_arrived()
     finish_pool(1)
-    x_pack(1)
+    x_pack_direct(1)
     forward_chunk(2)
     send_chunk(5)
-    x_final(0)
+    gram_second()
+    finish_pool(2)
+    x_pack_direct(2)
+    x_final_direct(0)
     z_start(0)
-    weights_arrived()
-    x_merge(1)
-    finish_pool(2)
-    x_pack(2)
-    gram_third()
     forward_chunk(3)
     send_chunk(6)
-    z_hop(0, 1)
-    x_final(1)
+    finish_pool(3)
+    x_pack_direct(3)
+    x_final_direct(1)
     z_start(1)
-    x_merge(2)
-    hess_piece(0, (z_at[7], z_at[1]), start=True)
-    finish_pool(3)
-    x_pack(3)
     forward_chunk(4)
     send_chunk(7)
-    z_hop(0, 2)
-    z_hop(1, 1)
-    x_final(2)
-    z_start(2)
-    hess_piece(0, (z_at[6], z_at[2]))
-    x_merge(3)
-    hess_piece(1, (z_at[7], z_at[1]))
+    z_hop(0, 1)
+    hess_piece(0, (z_at[7], z_at[1]), start=True)
     finish_pool(4)
     x_pack(4)
+    x_final_direct(2)
+    z_start(2)
     forward_chunk(5)
-    z_hop(0, 3)
-    z_hop(1, 2)
-    z_hop(2, 1)
-    hess_piece(0, (z_at[5], z_at[3]))
-    x_final(3)
-    z_start(3)
-    hess_piece(1, (z_at[6], z_at[2]))
-    x_merge(4)
-    hess_piece(2, (z_at[7], z_at[1]))
+    z_hop(1, 1)
+    hess_piece(1, (z_at[7], z_at[1]))
+    gram_third()
+    z_hop(0, 2)
+    hess_piece(0, (z_at[6], z_at[2]))
     finish_pool(5)
     x_pack(5)
-    gram_last()
-    rhs_start()
     forward_chunk(6)
-    z_hop(0, 4)
-    z_hop(1, 3)
-    z_hop(2, 2)
-    hess_piece(0, (z, z_at[4]))
-    z_hop(3, 1)
-    hess_piece(1, (z_at[5], z_at[3]))
-    x_final(4)
-    hess_piece(2, (z_at[6], z_at[2]))
-    x_merge(5)
-    hess_piece(3, (z_at[7], z_at[1]))
+    x_merge(4)
+    x_final_direct(3)
+    z_start(3)
+    z_hop(2, 1)
+    hess_piece(2, (z_at[7], z_at[1]))
+    z_hop(1, 2)
+    hess_piece(1, (z_at[6], z_at[2]))
     finish_pool(6)
     x_pack(6)
     forward_chunk(7)
-    z_hop(1, 4)
-    z_hop(2, 3)
-    z_hop(3, 2)
-    hess_piece(1, (z, z_at[4]))
-    hess_piece(2, (z_at[5], z_at[3]))
-    x_final(5)
-    hess_piece(3, (z_at[6], z_at[2]))
-    x_merge(6)
+    x_merge(5)
+    z_hop(0, 3)
+    hess_piece(0, (z_at[5], z_at[3]))
+    x_final(4)
+    z_hop(3, 1)
+    hess_piece(3, (z_at[7], z_at[1]))
     finish_pool(7)
     x_pack(7)
+    x_merge(6)
+    z_hop(2, 2)
+    hess_piece(2, (z_at[6], z_at[2]))
+    x_final(5)
+    gram_last()
+    rhs_start()
+    z_hop(1, 3)
+    hess_piece(1, (z_at[5], z_at[3]))
+    x_merge(7)
+    z_hop(0, 4)
+    hess_piece(0, (z, z_at[4]))
+    z_hop(3, 2)
+    hess_piece(3, (z_at[6], z_at[2]))
+    x_final(6)
+    z_hop(2, 3)
+    hess_piece(2, (z_at[5], z_at[3]))
+    x_final(7)
+    z_hop(1, 4)
+    grad_start()
+    z_hop(3, 3)
+    hess_piece(1, (z, z_at[4]))
     z_hop(2, 4)
-    z_hop(3, 3)
+    hess_piece(3, (z_at[5], z_at[3]))
     hess_piece(2, (z, z_at[4]))
-    hess_piece(3, (z_at[5], z_at[3]))
-    x_final(6)
-    x_merge(7)
     z_hop(3, 4)
     hess_piece(3, (z, z_at[4]), last=True)
-    x_final(7)
-    grad_start()
     own_systems()
     grad_last()
     join_systems()
@@ -494,7 +525,6 @@
 
 
 PANEL = 8
-RB = 32
 
 
 def lane_bcast(v, lane):
@@ -504,6 +534,13 @@
     while len(xs) > 1:
         xs = [xs[i] + xs[i+1] if i+1 < len(xs) else xs[i] for i in range(0, len(xs), 2)]
     return xs[0]
+
+def split(v):
+    h = v.astype(BF16)
+    rest = v - h.astype(F32)
+    m = rest.astype(BF16)
+    return h, m, (rest - m.astype(F32)).astype(BF16)
+
 
 def sweep_inverse(d, n):
     g = lambda i, j: d[(i, j) if i <= j else (j, i)]
@@ -543,19 +580,20 @@
         kept = [jnp.where(lane >= k0 + PANEL, r, 0.0) for r in rows]
         ws = [tree([dinv[(min(i, j), max(i, j))] * kept[j] for j in range(PANEL)]) for i in range(PANEL)]
         b = b - tree([lane_bcast(b, k0 + j) * ws[j] for j in range(PANEL)])
-        def update(base, count):
-            vs = [a_ref[pl.ds(base + q * NI, NI), :] for q in range(count)]
-            vs = [v - tree([lane_bcast(v, k0 + j) * ws[j] for j in range(PANEL)]) for v in vs]
-            for q in range(count):
-                a_ref[pl.ds(base + q * NI, NI), :] = vs[q]
-        left = KB - k0 - PANEL
-        if left % RB:
-            update((k0 + PANEL) * NI, left % RB)
-        if left // RB:
-            first = (k0 + PANEL + left % RB) // RB
-            @pl.loop(first, KB // RB)
-            def _(g):
-                update(pl.multiple_of(g * (RB * NI), RB * NI), RB)
+        first = (k0 + PANEL) * NI
+        rest = a_ref[first:, :]
+        count = KB * NI - first
+        at = lax.broadcasted_iota(jnp.int32, (count, KB), 1)
+        spread = jnp.take_along_axis(
+            rest, k0 + jnp.bitwise_and(jnp.right_shift(at, 3), PANEL - 1), axis=1, mode="promise_in_bounds")
+        item = jnp.bitwise_and(lax.broadcasted_iota(jnp.int32, (count, KB), 0), NI - 1)
+        spread = jnp.where(jnp.bitwise_and(at, NI - 1) == item, spread, 0.0)
+        h, m, l = split(spread)
+        wh, wm, wl = split(jnp.concatenate(ws, axis=0))
+        far = jnp.where(at < NI * PANEL, h.astype(F32), l.astype(F32)).astype(BF16)
+        a_ref[first:, :] = rest - jnp.dot(
+            jnp.concatenate([h, m, far], axis=1), jnp.concatenate([wh, wm, wh, wm, wl, wh], axis=0),
+            preferred_element_type=F32)
     x = jnp.zeros((NI, KB), F32)
     for p in range(KB // PANEL - 1, -1, -1):
         k0 = p * PANEL

time: 93.5 us -> 75.5 us (0.81)
  Pallas kernels: 92.3 us -> 75.1 us
    pallas_call x1, Pallas kernels: 21 us -> 10.3 us  [solve(): pl.pallas_call(solve_kernel, out_shape=jax.ShapeDtypeStruct((NI, KB), F32...]
    pallas_call x1, Pallas kernels: 71.3 us -> 64.9 us  [normal_equations(): pl.pallas_call(gather_kernel, out_shape=(jax.ShapeDtypeStruct((KB * NI, K...]
where the time goes in v3:
time: 75.5 us; the launch traced here: 75.3 us
  Pallas kernels  75.1 us (99%)
    pallas_call x1, Pallas kernels, normal_equations(): pl.pallas_call(gather_kernel, out_shape=(jax.ShapeDtypeStruct((KB * NI, K...  64.9 us
    pallas_call x1, Pallas kernels, solve(): pl.pallas_call(solve_kernel, out_shape=jax.ShapeDtypeStruct((NI, KB), F32...  10.3 us

profile of v3, /device:TPU:32, one launch (start us, length us, event | category | flops | bytes accessed | tf_op | source)
XLA Modules:
  0.0 75.3 jit_solution(6223399188172029838)
XLA Ops:
  0.0 64.9 %normal_equations.1 = (f32[1024,128]{1,0:T(8,128)}, f32[8,128]{1,0:T(8,128)}, f32[8,128]{1,0:T(8,128)}) custom-call(bf16[16,128,256]{2,1,0:T(8,128)(2,1)} %bitcast.4, s32[1,8]{1,0:T(1,128)} %bitcast.7, bf16[128,256]{1,0:T(8,128)(2,1)} %item_ref.1, bf16[8,128,128]{2,1,0:T(8,128)(2,1)} %bitcast.5, bf16[8,128,128]{2,1,0:T(8,128)(2,1)} %bitcast.6), custom_call_target="tpu_custom_call" | custom-call | tf_op jit(solution)/shard_map/normal_equations/pallas_call | solution.py:476
  64.9 10.3 %block_solve.1 = f32[8,128]{1,0:T(8,128)} custom-call(f32[1024,128]{1,0:T(8,128)} %get-tuple-element.8.system_ref, f32[8,128]{1,0:T(8,128)} %get-tuple-element.9.rhs_ref, f32[8,128]{1,0:T(8,128)} %get-tuple-element.10.mine_ref), custom_call_target="tpu_custom_call" | custom-call | tf_op jit(solution)/shard_map/block_solve/pallas_call | solution.py:611

commit v4 on v3

--- a/solution.py
+++ b/solution.py
@@ -22,6 +22,8 @@
 NCH = 2 * NQ
 CU = NT * ROWS
 NZ = 8
+STEPS = 32000.0
+TINY = 1e-18
 BOTH_LAST = (((1,), (1,)), ((), ()))
 BOTH_FIRST = (((0,), (0,)), ((), ()))
 
@@ -30,7 +32,7 @@
     user_ref, tile_ref, item_ref, weight_ref, target_ref,
     system_ref, rhs_ref, mine_ref,
     pools, far_a, far_b, out_p, out_m, in_a, in_b, in_p, in_m, rights, zbufs,
-    reqs, item, itemf, weight, target, wt_own, tt_own, wz, hacc, hsend, hin, hown, gsend, gin,
+    reqs, item, itemf, weight, target, wt_own, tt_own, wz, hacc, hsend, hin, dsend, din, hown, gsend, gin,
     gpart, gin1, gone, gin2, gtwo, gall, local_sem, send_sem, recv_sem,
 ):
     me_b, me_g = lax.axis_index("blk"), lax.axis_index("grp")
@@ -69,6 +71,25 @@
             src_ref=dst, dst_ref=dst, send_sem=send_sem.at[k], recv_sem=recv_sem.at[k],
             device_id=sibling, device_id_type=MESH).wait_recv()
 
+    def send_all(name, pairs):
+        k = slot(name)
+        for src, dst, device in pairs:
+            copy = pltpu.make_async_remote_copy(
+                src_ref=src, dst_ref=dst, send_sem=send_sem.at[k], recv_sem=recv_sem.at[k],
+                device_id=device, device_id_type=MESH)
+            copy.start()
+
+    def all_of(name, whole):
+        k = slot(name)
+        return pltpu.make_async_remote_copy(
+            src_ref=whole, dst_ref=whole, send_sem=send_sem.at[k], recv_sem=recv_sem.at[k],
+            device_id=sibling, device_id_type=MESH)
+
+    def all_arrived(name, whole):
+        copy = all_of(name, whole)
+        copy.wait_recv()
+        sent.append(copy)
+
     locals_ = {}
 
     def fetch(name, src, dst):
@@ -196,22 +217,23 @@
             rights[c - NQ][j, :half] = first
             rights[c - NQ][j, half:] = second
 
+    def slots_of(q, source, part):
+        return zbufs[q].at[source, pl.ds(part * (NT // 2), NT // 2)]
+
     def z_start(q):
-        send(("zr", q, 1), zbufs[q].at[z], zbufs[q].at[z], z_peer[1])
-        send(("zl", q, 1), zbufs[q].at[z], zbufs[q].at[z], z_peer[7])
+        for first in (0, 1):
+            for side, part, peer in (("zr", first, z_peer[1]), ("zl", 1 - first, z_peer[7])):
+                mine = slots_of(q, z, part)
+                send((side, q, 1, part), mine, mine, peer)
 
     def z_hop(q, h):
-        if h < 4:
-            from_left, from_right = z_at[NZ - h], z_at[h]
-            arrived(("zr", q, h), zbufs[q].at[from_left])
-            part = zbufs[q].at[from_left] if h < 3 else zbufs[q].at[from_left, pl.ds(0, NT // 2)]
-            send(("zr", q, h + 1), part, part, z_peer[1])
-            arrived(("zl", q, h), zbufs[q].at[from_right])
-            part = zbufs[q].at[from_right] if h < 3 else zbufs[q].at[from_right, pl.ds(NT // 2, NT // 2)]
-            send(("zl", q, h + 1), part, part, z_peer[7])
-        else:
-            arrived(("zr", q, 4), zbufs[q].at[z_at[4], pl.ds(0, NT // 2)])
-            arrived(("zl", q, 4), zbufs[q].at[z_at[4], pl.ds(NT // 2, NT // 2)])
+        for first in (0, 1) if h < 4 else (0,):
+            for side, part, source, peer in (
+                ("zr", first, z_at[NZ - h], z_peer[1]), ("zl", 1 - first, z_at[h], z_peer[7])):
+                here = slots_of(q, source, part)
+                arrived((side, q, h, part), here)
+                if h < 3 or (h == 3 and first == 0):
+                    send((side, q, h + 1, part), here, here, peer)
 
     def transposed(ref, out):
         span = TILE // ROWS
@@ -223,13 +245,11 @@
     def send_weights():
         locals_["weight"].wait()
         transposed(weight, wt_own)
-        for k in range(1, NZ):
-            send(("w", k), wt_own.at[z_at[k]], wz.at[z], z_peer[k])
+        send_all("w", [(wt_own.at[z_at[k]], wz.at[z], z_peer[k]) for k in range(1, NZ)])
         wz[z] = wt_own[z]
 
     def weights_arrived():
-        for k in range(1, NZ):
-            arrived(("w", k), wz.at[z_at[NZ - k]])
+        all_arrived("w", wz.at[pl.ds(0, NZ - 1)])
 
     def gram_start():
         left = jnp.zeros((KB, KB), F32)
@@ -241,29 +261,23 @@
             right += lax.dot_general(a, b, BOTH_FIRST, preferred_element_type=F32)
         gpart[:, 0] = left.reshape(16, 8, KB)
         gpart[:, 1] = right.reshape(16, 8, KB)
-        for k in range(1, 16):
-            send(("g1", k), gpart.at[blk_at[k]], gin1.at[me_b], blk_peer[k])
+        send_all("g1", [(gpart.at[blk_at[k]], gin1.at[me_b], blk_peer[k]) for k in range(1, 16)])
         gin1[me_b] = gpart[me_b]
 
     def gram_second():
-        for k in range(1, 16):
-            arrived(("g1", k), gin1.at[blk_at[16 - k]])
+        all_arrived("g1", gin1.at[pl.ds(0, 15)])
         gone[...] = jnp.sum(gin1[...], axis=0)
-        for k in range(1, 16):
-            send(("g2", k), gone, gin2.at[me_g], grp_peer[k])
+        send_all("g2", [(gone, gin2.at[me_g], grp_peer[k]) for k in range(1, 16)])
         gin2[me_g] = gone[...]
 
     def gram_third():
-        for k in range(1, 16):
-            arrived(("g2", k), gin2.at[grp_at[16 - k]])
+        all_arrived("g2", gin2.at[pl.ds(0, 15)])
         gtwo[...] = jnp.sum(gin2[...], axis=0)
-        for k in range(1, 16):
-            send(("g3", k), gtwo, gall.at[me_b], blk_peer[k])
+        send_all("g3", [(gtwo, gall.at[me_b], blk_peer[k]) for k in range(1, 16)])
         gall[me_b] = gtwo[...]
 
     def gram_last():
-        for k in range(1, 16):
-            arrived(("g3", k), gall.at[blk_at[16 - k]])
+        all_arrived("g3", gall.at[pl.ds(0, 15)])
 
     GROUP = 4
 
@@ -296,12 +310,30 @@
     def row_col():
         return (lax.broadcasted_iota(jnp.int32, (KB, KB), 0), lax.broadcasted_iota(jnp.int32, (KB, KB), 1))
 
+    def diagonal(square):
+        row, col = row_col()
+        kept = jnp.where(row == col, square, 0.0)
+        return jnp.sum(kept, axis=0, keepdims=True), jnp.sum(kept, axis=1, keepdims=True)
+
+    def inverse_root(d):
+        root = jnp.sqrt(d)
+        return jnp.where(root > TINY, 1.0 / jnp.maximum(root, TINY), 0.0)
+
     def fold(i):
         row, col = row_col()
-        hsend[i // 2, :KB] = jnp.where(row <= col, hacc[i], hacc[i + 1])
-        diag = jnp.sum(jnp.where(row == col, hacc[i + 1], 0.0), axis=0, keepdims=True)
-        hsend[i // 2, KB:] = jnp.broadcast_to(diag, (8, KB))
+        upper, lower = hacc[i], hacc[i + 1]
+        upper_row, upper_col = diagonal(upper)
+        lower_row, lower_col = diagonal(lower)
+        square = jnp.where(row <= col, upper, lower)
+        by_col = jnp.where(row <= col, inverse_root(upper_col), inverse_root(lower_col))
+        by_row = jnp.where(row <= col, inverse_root(upper_row), inverse_root(lower_row))
+        coded = jnp.round(square * by_col * by_row * STEPS)
+        coded = jnp.minimum(jnp.maximum(coded, -32767.0), 32767.0)
+        hsend[i // 2] = coded.astype(jnp.int32).astype(jnp.int16)
+        first = lax.broadcasted_iota(jnp.int32, (8, KB), 0) == 0
+        dsend[i // 2] = jnp.where(first, upper_row, lower_row)
         send(("h", i), hsend.at[i // 2], hin.at[i // 2], partner)
+        send(("d", i), dsend.at[i // 2], din.at[i // 2], partner)
 
     def own_systems():
         prior = PRIOR * gall[:, 0].reshape(KB, KB)
@@ -312,14 +344,25 @@
     def join_systems():
         row, col = row_col()
         for i in range(0, NI, 2):
+            arrived(("d", i), din.at[i // 2])
+            upper_row, lower_row = din[i // 2, 0:1], din[i // 2, 1:2]
+            upper_root, lower_root = jnp.sqrt(upper_row), jnp.sqrt(lower_row)
+            as_col = lambda r: jnp.sum(jnp.where(row == col, r, 0.0), axis=1, keepdims=True)
+            by_col = jnp.where(row <= col, as_col(upper_root), as_col(lower_root))
+            by_row = jnp.where(row <= col, upper_root, lower_root)
+            scale = by_col * by_row * (1.0 / STEPS)
             arrived(("h", i), hin.at[i // 2])
-            square = hin[i // 2, :KB]
+            square = hin[i // 2].astype(jnp.int32).astype(F32) * scale
             turned = square.T
-            diag = hin[i // 2, KB:KB + 1]
-            first = jnp.where(row <= col, square, turned)
-            second = jnp.where(row > col, square, jnp.where(row == col, diag, turned))
+            first = jnp.where(row < col, square, jnp.where(row == col, upper_row, turned))
+            second = jnp.where(row > col, square, jnp.where(row == col, lower_row, turned))
             system_ref[pl.ds(i, KB, stride=NI), :] = hown[i] + first
             system_ref[pl.ds(i + 1, KB, stride=NI), :] = hown[i + 1] + second
+
+    def drain():
+        for copy in sent:
+            copy.wait_send()
+        sent.clear()
 
     def grad_start():
         total = jnp.zeros((TILE, KB), F32)
@@ -334,8 +377,7 @@
             resid = (w * (pred - t)).astype(BF16)
             total += jnp.dot(resid, left, preferred_element_type=F32)
         gsend[...] = total.reshape(16, NI, KB)
-        for k in range(1, 16):
-            send(("gr", k), gsend.at[grp_at[k]], gin.at[me_g], grp_peer[k])
+        send_all("gr", [(gsend.at[grp_at[k]], gin.at[me_g], grp_peer[k]) for k in range(1, 16)])
         gin[me_g] = gsend[me_g]
 
     def rhs_start():
@@ -350,8 +392,7 @@
                               precision=exact, preferred_element_type=F32))
 
     def grad_last():
-        for k in range(1, 16):
-            arrived(("gr", k), gin.at[grp_at[16 - k]])
+        all_arrived("gr", gin.at[pl.ds(0, 15)])
         rhs_ref[...] += jnp.sum(gin[...], axis=0)
 
     def target_ready():
@@ -389,26 +430,25 @@
     gram_second()
     finish_pool(2)
     x_pack_direct(2)
+    forward_chunk(3)
+    send_chunk(6)
     x_final_direct(0)
     z_start(0)
-    forward_chunk(3)
-    send_chunk(6)
+    x_final_direct(1)
+    z_start(1)
     finish_pool(3)
     x_pack_direct(3)
-    x_final_direct(1)
-    z_start(1)
     forward_chunk(4)
     send_chunk(7)
     z_hop(0, 1)
     hess_piece(0, (z_at[7], z_at[1]), start=True)
     finish_pool(4)
     x_pack(4)
+    forward_chunk(5)
     x_final_direct(2)
     z_start(2)
-    forward_chunk(5)
     z_hop(1, 1)
     hess_piece(1, (z_at[7], z_at[1]))
-    gram_third()
     z_hop(0, 2)
     hess_piece(0, (z_at[6], z_at[2]))
     finish_pool(5)
@@ -419,39 +459,40 @@
     z_start(3)
     z_hop(2, 1)
     hess_piece(2, (z_at[7], z_at[1]))
-    z_hop(1, 2)
-    hess_piece(1, (z_at[6], z_at[2]))
+    gram_third()
     finish_pool(6)
     x_pack(6)
     forward_chunk(7)
     x_merge(5)
+    z_hop(1, 2)
+    hess_piece(1, (z_at[6], z_at[2]))
+    x_final(4)
     z_hop(0, 3)
     hess_piece(0, (z_at[5], z_at[3]))
-    x_final(4)
     z_hop(3, 1)
-    hess_piece(3, (z_at[7], z_at[1]))
     finish_pool(7)
     x_pack(7)
     x_merge(6)
+    hess_piece(3, (z_at[7], z_at[1]))
     z_hop(2, 2)
     hess_piece(2, (z_at[6], z_at[2]))
     x_final(5)
-    gram_last()
-    rhs_start()
     z_hop(1, 3)
     hess_piece(1, (z_at[5], z_at[3]))
     x_merge(7)
     z_hop(0, 4)
     hess_piece(0, (z, z_at[4]))
+    x_final(6)
     z_hop(3, 2)
     hess_piece(3, (z_at[6], z_at[2]))
-    x_final(6)
     z_hop(2, 3)
+    x_final(7)
+    grad_start()
+    z_hop(1, 4)
     hess_piece(2, (z_at[5], z_at[3]))
-    x_final(7)
-    z_hop(1, 4)
-    grad_start()
     z_hop(3, 3)
+    gram_last()
+    rhs_start()
     hess_piece(1, (z, z_at[4]))
     z_hop(2, 4)
     hess_piece(3, (z_at[5], z_at[3]))
@@ -459,6 +500,7 @@
     z_hop(3, 4)
     hess_piece(3, (z, z_at[4]), last=True)
     own_systems()
+    drain()
     grad_last()
     join_systems()
     for copy in sent:
@@ -466,7 +508,7 @@
     assert len(slots) <= NSEM, len(slots)
 
 
-NSEM = 260
+NSEM = 240
 
 
 def normal_equations(user_factors, item_factors, tile_user, tile_weight, tile_target):
@@ -503,8 +545,10 @@
             vm((NZ, 16, NT * TILE), BF16),
             vm((NZ, 16, NT * TILE), BF16),
             vm((16, KB, KB), F32),
-            vm((NI // 2, KB + 8, KB), F32),
-            vm((NI // 2, KB + 8, KB), F32),
+            vm((NI // 2, KB, KB), jnp.int16),
+            vm((NI // 2, KB, KB), jnp.int16),
+            vm((NI // 2, 8, KB), F32),
+            vm((NI // 2, 8, KB), F32),
             vm((NI, KB, KB), F32),
             vm((16, NI, KB), F32),
             vm((16, NI, KB), F32),

time: 75.5 us -> 73.2 us (0.970)
  Pallas kernels: 75.1 us -> 72.2 us
    pallas_call x1, Pallas kernels: 64.9 us -> 62 us  [normal_equations(): pl.pallas_call(gather_kernel, out_shape=(jax.ShapeDtypeStruct((KB * NI, K...]
where the time goes in v4:
time: 73.2 us; the launch traced here: 72.4 us
  Pallas kernels  72.2 us (99%)
    pallas_call x1, Pallas kernels, normal_equations(): pl.pallas_call(gather_kernel, out_shape=(jax.ShapeDtypeStruct((KB * NI, K...  62 us
    pallas_call x1, Pallas kernels, solve(): pl.pallas_call(solve_kernel, out_shape=jax.ShapeDtypeStruct((NI, KB), F32...  10.3 us

profile of v4, /device:TPU:32, one launch (start us, length us, event | category | flops | bytes accessed | tf_op | source)
XLA Modules:
  0.0 72.4 jit_solution(15517382726938502404)
XLA Ops:
  0.0 62.0 %normal_equations.1 = (f32[1024,128]{1,0:T(8,128)}, f32[8,128]{1,0:T(8,128)}, f32[8,128]{1,0:T(8,128)}) custom-call(bf16[16,128,256]{2,1,0:T(8,128)(2,1)} %bitcast.4, s32[1,8]{1,0:T(1,128)} %bitcast.7, bf16[128,256]{1,0:T(8,128)(2,1)} %item_ref.1, bf16[8,128,128]{2,1,0:T(8,128)(2,1)} %bitcast.5, bf16[8,128,128]{2,1,0:T(8,128)(2,1)} %bitcast.6), custom_call_target="tpu_custom_call" | custom-call | tf_op jit(solution)/shard_map/normal_equations/pallas_call | solution.py:518
  62.0 10.3 %block_solve.1 = f32[8,128]{1,0:T(8,128)} custom-call(f32[1024,128]{1,0:T(8,128)} %get-tuple-element.8.system_ref, f32[8,128]{1,0:T(8,128)} %get-tuple-element.9.rhs_ref, f32[8,128]{1,0:T(8,128)} %get-tuple-element.10.mine_ref), custom_call_target="tpu_custom_call" | custom-call | tf_op jit(solution)/shard_map/block_solve/pallas_call | solution.py:655

commit v5 on v4

--- a/solution.py
+++ b/solution.py
@@ -22,6 +22,7 @@
 NCH = 2 * NQ
 CU = NT * ROWS
 NZ = 8
+PANEL = 8
 STEPS = 32000.0
 TINY = 1e-18
 BOTH_LAST = (((1,), (1,)), ((), ()))
@@ -30,10 +31,10 @@
 
 def gather_kernel(
     user_ref, tile_ref, item_ref, weight_ref, target_ref,
-    system_ref, rhs_ref, mine_ref,
+    out_ref,
     pools, far_a, far_b, out_p, out_m, in_a, in_b, in_p, in_m, rights, zbufs,
     reqs, item, itemf, weight, target, wt_own, tt_own, wz, hacc, hsend, hin, dsend, din, hown, gsend, gin,
-    gpart, gin1, gone, gin2, gtwo, gall, local_sem, send_sem, recv_sem,
+    gpart, gin1, gone, gin2, gtwo, gall, system_ref, rhs_ref, mine_ref, dinv_ref, local_sem, send_sem, recv_sem,
 ):
     me_b, me_g = lax.axis_index("blk"), lax.axis_index("grp")
     y_lo, x, core = me_b // 8, lax.rem(me_b // 2, 4), lax.rem(me_b, 2)
@@ -97,23 +98,27 @@
         copy.start()
         locals_[name] = copy
 
+    fetch("tile", tile_ref, reqs.at[x])
+    for c in range(NCH):
+        rows, cols = (c % NQ) * ROWS, (c // NQ) * KB
+        fetch(("pool", c), user_ref.at[:, pl.ds(rows, ROWS), pl.ds(cols, KB)], pools[c].at[own])
+    fetch("weight", weight_ref, weight)
+    fetch("target", target_ref, target)
+    fetch("item", item_ref, item)
+
     barrier = pltpu.get_barrier_semaphore()
     for k in range(1, 16):
         pl.semaphore_signal(barrier, inc=1, device_id=blk_peer[k], device_id_type=MESH)
         pl.semaphore_signal(barrier, inc=1, device_id=grp_peer[k], device_id_type=MESH)
-    for c in range(NCH):
-        rows, cols = (c % NQ) * ROWS, (c // NQ) * KB
-        fetch(("pool", c), user_ref.at[:, pl.ds(rows, ROWS), pl.ds(cols, KB)], pools[c].at[own])
-    fetch("tile", tile_ref, reqs.at[x])
-    fetch("weight", weight_ref, weight)
-    fetch("target", target_ref, target)
-    fetch("item", item_ref, item)
-
-    for name in [("pool", c) for c in range(NCH)] + ["tile"]:
-        locals_[name].wait()
+
+    def fetched(name):
+        if name in locals_:
+            locals_.pop(name).wait()
+
     pl.semaphore_wait(barrier, 30)
 
     def send_chunk(c):
+        fetched(("pool", c))
         send(("y", c), pools[c].at[own], pools[c].at[own], y_peer)
         send(("s", c), pools[c].at[own], pools[c].at[own], sibling)
 
@@ -140,44 +145,6 @@
     half = ROWS // 2
 
     def x_pack(c):
-        for j in range(NT):
-            v = pick(c, wanted(2, j))
-            far_a[c][j] = v[:half]
-            far_b[c][j] = v[half:]
-        send(("xa", c), far_a[c], in_a[c], x_peer[1])
-        send(("xb", c), far_b[c], in_b[c], x_peer[3])
-        for j in range(NT):
-            out_p[c][1, j] = pick(c, wanted(1, j))[half:]
-            out_m[c][0, j] = pick(c, wanted(3, j))[:half]
-        send(("p1", c), out_p[c].at[1], in_m[c].at[1], x_peer[1])
-        send(("m0", c), out_m[c].at[0], in_p[c].at[0], x_peer[3])
-
-    def x_merge(c):
-        arrived(("xa", c), in_a[c])
-        for j in range(NT):
-            t = wanted(1, j)
-            out_p[c][0, j] = jnp.where(column(t) == x, pick(c, t)[:half], in_a[c][j])
-        send(("p0", c), out_p[c].at[0], in_m[c].at[0], x_peer[1])
-        arrived(("xb", c), in_b[c])
-        for j in range(NT):
-            t = wanted(3, j)
-            out_m[c][1, j] = jnp.where(column(t) == x, pick(c, t)[half:], in_b[c][j])
-        send(("m1", c), out_m[c].at[1], in_p[c].at[1], x_peer[3])
-
-    def x_final(c):
-        arrived(("p1", c), in_m[c].at[1])
-        arrived(("m0", c), in_p[c].at[0])
-        arrived(("p0", c), in_m[c].at[0])
-        arrived(("m1", c), in_p[c].at[1])
-        for j in range(NT):
-            t = wanted(0, j)
-            away = jnp.bitwise_and(column(t) - x + 4, 3)
-            mine = pick(c, t)
-            first = jnp.where(away == 0, mine[:half], jnp.where(away == 1, in_p[c][0, j], in_m[c][0, j]))
-            second = jnp.where(away == 0, mine[half:], jnp.where(away == 3, in_m[c][1, j], in_p[c][1, j]))
-            put(c, j, first, second)
-
-    def x_pack_direct(c):
         for j in range(NT):
             v = pick(c, wanted(2, j))
             far_a[c][j] = v[:half]
@@ -194,7 +161,7 @@
         send(("p0", c), out_p[c], in_m[c], x_peer[1])
         send(("m0", c), out_m[c], in_p[c], x_peer[3])
 
-    def x_final_direct(c):
+    def x_final(c):
         arrived(("p0", c), in_m[c])
         arrived(("m0", c), in_p[c])
         arrived(("xa", c), in_a[c])
@@ -243,7 +210,7 @@
                 out[:, :, pl.ds((q * (NT // span) + p) * TILE, TILE)] = block.T.reshape(NZ, 16, TILE)
 
     def send_weights():
-        locals_["weight"].wait()
+        fetched("weight")
         transposed(weight, wt_own)
         send_all("w", [(wt_own.at[z_at[k]], wz.at[z], z_peer[k]) for k in range(1, NZ)])
         wz[z] = wt_own[z]
@@ -252,6 +219,8 @@
         all_arrived("w", wz.at[pl.ds(0, NZ - 1)])
 
     def gram_start():
+        for c in range(NCH):
+            fetched(("pool", c))
         left = jnp.zeros((KB, KB), F32)
         right = jnp.zeros((KB, KB), F32)
         for q in range(NQ):
@@ -364,19 +333,21 @@
             copy.wait_send()
         sent.clear()
 
+    def grad_part(q):
+        left = zbufs[q][z].reshape(CU, KB)
+        right = rights[q][...].reshape(CU, KB)
+        pred = lax.dot_general(item[:, :KB], left, BOTH_LAST, preferred_element_type=F32)
+        pred += lax.dot_general(item[:, KB:], right, BOTH_LAST, preferred_element_type=F32)
+        w = wt_own[:, :, pl.ds(q * CU, CU)].reshape(TILE, CU).astype(F32)
+        t = tt_own[:, :, pl.ds(q * CU, CU)].reshape(TILE, CU).astype(F32)
+        resid = (w * (pred - t)).astype(BF16)
+        part = jnp.dot(resid, left, preferred_element_type=F32).reshape(16, NI, KB)
+        if q == 0:
+            gsend[...] = part
+        else:
+            gsend[...] += part
+
     def grad_start():
-        total = jnp.zeros((TILE, KB), F32)
-        items = item[...]
-        for q in range(NQ):
-            left = zbufs[q][z].reshape(CU, KB)
-            right = rights[q][...].reshape(CU, KB)
-            pred = lax.dot_general(items[:, :KB], left, BOTH_LAST, preferred_element_type=F32)
-            pred += lax.dot_general(items[:, KB:], right, BOTH_LAST, preferred_element_type=F32)
-            w = wt_own[:, :, pl.ds(q * CU, CU)].reshape(TILE, CU).astype(F32)
-            t = tt_own[:, :, pl.ds(q * CU, CU)].reshape(TILE, CU).astype(F32)
-            resid = (w * (pred - t)).astype(BF16)
-            total += jnp.dot(resid, left, preferred_element_type=F32)
-        gsend[...] = total.reshape(16, NI, KB)
         send_all("gr", [(gsend.at[grp_at[k]], gin.at[me_g], grp_peer[k]) for k in range(1, 16)])
         gin[me_g] = gsend[me_g]
 
@@ -396,11 +367,12 @@
         rhs_ref[...] += jnp.sum(gin[...], axis=0)
 
     def target_ready():
-        locals_["target"].wait()
+        fetched("target")
         transposed(target, tt_own)
-        locals_["item"].wait()
+        fetched("item")
 
     def send_requests():
+        fetched("tile")
         for k in range(1, 4):
             send(("rq", k), reqs.at[x], reqs.at[x], x_peer[k])
 
@@ -419,25 +391,25 @@
     send_chunk(3)
     requests_arrived()
     finish_pool(0)
-    x_pack_direct(0)
+    x_pack(0)
     forward_chunk(1)
     send_chunk(4)
     weights_arrived()
     finish_pool(1)
-    x_pack_direct(1)
+    x_pack(1)
     forward_chunk(2)
     send_chunk(5)
     gram_second()
     finish_pool(2)
-    x_pack_direct(2)
+    x_pack(2)
     forward_chunk(3)
     send_chunk(6)
-    x_final_direct(0)
+    x_final(0)
     z_start(0)
-    x_final_direct(1)
+    x_final(1)
     z_start(1)
     finish_pool(3)
-    x_pack_direct(3)
+    x_pack(3)
     forward_chunk(4)
     send_chunk(7)
     z_hop(0, 1)
@@ -445,7 +417,7 @@
     finish_pool(4)
     x_pack(4)
     forward_chunk(5)
-    x_final_direct(2)
+    x_final(2)
     z_start(2)
     z_hop(1, 1)
     hess_piece(1, (z_at[7], z_at[1]))
@@ -454,8 +426,7 @@
     finish_pool(5)
     x_pack(5)
     forward_chunk(6)
-    x_merge(4)
-    x_final_direct(3)
+    x_final(3)
     z_start(3)
     z_hop(2, 1)
     hess_piece(2, (z_at[7], z_at[1]))
@@ -463,30 +434,31 @@
     finish_pool(6)
     x_pack(6)
     forward_chunk(7)
-    x_merge(5)
+    x_final(4)
     z_hop(1, 2)
+    grad_part(0)
+    z_hop(0, 3)
     hess_piece(1, (z_at[6], z_at[2]))
-    x_final(4)
-    z_hop(0, 3)
     hess_piece(0, (z_at[5], z_at[3]))
     z_hop(3, 1)
     finish_pool(7)
     x_pack(7)
-    x_merge(6)
     hess_piece(3, (z_at[7], z_at[1]))
+    x_final(5)
     z_hop(2, 2)
+    grad_part(1)
     hess_piece(2, (z_at[6], z_at[2]))
-    x_final(5)
     z_hop(1, 3)
     hess_piece(1, (z_at[5], z_at[3]))
-    x_merge(7)
+    x_final(6)
     z_hop(0, 4)
+    grad_part(2)
     hess_piece(0, (z, z_at[4]))
-    x_final(6)
     z_hop(3, 2)
     hess_piece(3, (z_at[6], z_at[2]))
+    x_final(7)
     z_hop(2, 3)
-    x_final(7)
+    grad_part(3)
     grad_start()
     z_hop(1, 4)
     hess_piece(2, (z_at[5], z_at[3]))
@@ -506,9 +478,10 @@
     for copy in sent:
         copy.wait_send()
     assert len(slots) <= NSEM, len(slots)
-
-
-NSEM = 240
+    solve(system_ref, rhs_ref, mine_ref, out_ref, dinv_ref)
+
+
+NSEM = 180
 
 
 def normal_equations(user_factors, item_factors, tile_user, tile_weight, tile_target):
@@ -517,13 +490,9 @@
     both = (2,) + chunk
     return pl.pallas_call(
         gather_kernel,
-        out_shape=(
-            jax.ShapeDtypeStruct((KB * NI, KB), F32),
-            jax.ShapeDtypeStruct((NI, KB), F32),
-            jax.ShapeDtypeStruct((NI, KB), F32),
-        ),
+        out_shape=jax.ShapeDtypeStruct((NI, KB), F32),
         in_specs=[pl.BlockSpec(memory_space=pl.ANY)] * 5,
-        out_specs=(pl.BlockSpec(memory_space=pltpu.VMEM),) * 3,
+        out_specs=pl.BlockSpec(memory_space=pltpu.VMEM),
         scratch_shapes=[
             [vm((4, OWN, ROWS, KB), BF16)] * NCH,
             [vm(chunk, BF16)] * NCH,
@@ -558,6 +527,10 @@
             vm((16, 2, 8, KB), F32),
             vm((2, 8, KB), F32),
             vm((16, 2, 8, KB), F32),
+            vm((KB * NI, KB), F32),
+            vm((NI, KB), F32),
+            vm((NI, KB), F32),
+            vm((KB // PANEL, PANEL * (PANEL + 1) // 2, NI, KB), F32),
             pltpu.SemaphoreType.DMA((NCH + 4,)),
             pltpu.SemaphoreType.DMA((NSEM,)),
             pltpu.SemaphoreType.DMA((NSEM,)),
@@ -566,9 +539,6 @@
             collective_id=0, has_side_effects=True, vmem_limit_bytes=60 * 1024 * 1024),
         name="normal_equations",
     )(user_factors, tile_user, item_factors, tile_weight, tile_target)
-
-
-PANEL = 8
 
 
 def lane_bcast(v, lane):
@@ -606,12 +576,9 @@
         g = lambda i, j, d=d: d[(i, j) if i <= j else (j, i)]
     return {ij: -v for ij, v in d.items()}
 
-def solve_kernel(system_ref, rhs_ref, mine_ref, out_ref, a_ref, dinv_ref, sem):
-    load = pltpu.make_async_copy(system_ref, a_ref, sem)
-    load.start()
+def solve(a_ref, rhs_ref, mine_ref, out_ref, dinv_ref):
     lane = lax.broadcasted_iota(jnp.int32, (NI, KB), 1)
     b = rhs_ref[...]
-    load.wait()
     pairs = [(i, j) for i in range(PANEL) for j in range(i, PANEL)]
     for p in range(KB // PANEL):
         k0 = p * PANEL
@@ -650,26 +617,10 @@
             b = b - tree([xs[j] * jnp.where(lane < k0, a_ref[pl.ds((k0 + j) * NI, NI), :], 0.0) for j in range(PANEL)])
     out_ref[...] = mine_ref[...] - x
 
-def solve(system, rhs, mine):
-    vmem = pl.BlockSpec(memory_space=pltpu.VMEM)
-    return pl.pallas_call(
-        solve_kernel,
-        out_shape=jax.ShapeDtypeStruct((NI, KB), F32),
-        in_specs=[pl.BlockSpec(memory_space=pl.ANY), vmem, vmem],
-        out_specs=vmem,
-        scratch_shapes=[
-            pltpu.VMEM((KB * NI, KB), F32),
-            pltpu.VMEM((KB // PANEL, PANEL * (PANEL + 1) // 2, NI, KB), F32),
-            pltpu.SemaphoreType.DMA,
-        ],
-        compiler_params=pltpu.CompilerParams(vmem_limit_bytes=60 * 1024 * 1024),
-        name="block_solve",
-    )(system, rhs, mine)
-
 
 def local(user_factors, item_factors, tile_user, tile_weight, tile_target):
-    return solve(*normal_equations(
-        user_factors.reshape(OWN, TILE, K), item_factors, tile_user[0], tile_weight[0, 0], tile_target[0, 0]))
+    return normal_equations(
+        user_factors.reshape(OWN, TILE, K), item_factors, tile_user[0], tile_weight[0, 0], tile_target[0, 0])
 
 
 def solution(mesh):

time: 73.2 us -> 70.6 us (0.964)
  Pallas kernels: 72.2 us -> 69.2 us
  local copies, waits for them, and re-layouts: 0 us -> 1.28 us
    pallas_call x2 -> x1, Pallas kernels: 72.2 us -> 69.2 us  [normal_equations(): pl.pallas_call(gather_kernel, out_shape=jax.ShapeDtypeStruct((NI, KB), F3...]
    unnamed x0 -> x1, local copies, waits for them, and re-layouts: none -> 1.28 us
where the time goes in v5:
time: 70.6 us; the launch traced here: 70.5 us
  Pallas kernels  69.2 us (98%)
  local copies, waits for them, and re-layouts  1.28 us (2%)
    pallas_call x1, Pallas kernels, normal_equations(): pl.pallas_call(gather_kernel, out_shape=jax.ShapeDtypeStruct((NI, KB), F3...  69.2 us

profile of v5, /device:TPU:32, one launch (start us, length us, event | category | flops | bytes accessed | tf_op | source)
XLA Modules:
  0.0 70.5 jit_solution(11463354562832035372)
XLA Ops:
  0.0 69.2 %normal_equations.1 = f32[8,128]{1,0:T(8,128)} custom-call(bf16[16,128,256]{2,1,0:T(8,128)(2,1)} %bitcast.4, s32[1,8]{1,0:T(1,128)} %bitcast.7, bf16[128,256]{1,0:T(8,128)(2,1)} %item_ref.1, bf16[8,128,128]{2,1,0:T(8,128)(2,1)} %bitcast.5, bf16[8,128,128]{2,1,0:T(8,128)(2,1)} %bitcast.6), custom_call_target="tpu_custom_call" | custom-call | tf_op jit(solution)/shard_map/normal_equations/pallas_call | solution.py:491
  69.2 1.3 %copy.7 = f32[8,128]{1,0:T(8,128)} copy(f32[8,128]{1,0:T(8,128)} %normal_equations.1) | data formatting | bytes 8192

commit v6 on v5

--- a/solution.py
+++ b/solution.py
@@ -248,8 +248,6 @@
     def gram_last():
         all_arrived("g3", gall.at[pl.ds(0, 15)])
 
-    GROUP = 4
-
     def hess_piece(q, sources, start=False, last=False):
         users = [zbufs[q][s].reshape(CU, KB) for s in sources]
         users_t = jnp.concatenate(
@@ -261,19 +259,20 @@
         theirs = jnp.where(y_hi == 0, scale[8:], scale[:8])
         ours = jnp.where(y_hi == 0, scale[:8], scale[8:])
         scale = jnp.concatenate([theirs, ours], axis=0)
-        for i0 in range(0, 16, GROUP):
+        group = 4 if last else 8
+        for i0 in range(0, 16, group):
             lhs = []
-            for i in range(i0, i0 + GROUP):
+            for i in range(i0, i0 + group):
                 row = jnp.broadcast_to(scale[i:i + 1], (16, width)).astype(BF16)
                 lhs.append((row[None] * users_t).reshape(KB, width))
             part = jnp.dot(jnp.concatenate(lhs, axis=0), users, preferred_element_type=F32)
-            part = part.reshape(GROUP, KB, KB)
+            part = part.reshape(group, KB, KB)
             if start:
-                hacc[i0:i0 + GROUP] = part
+                hacc[i0:i0 + group] = part
             else:
-                hacc[i0:i0 + GROUP] += part
+                hacc[i0:i0 + group] += part
             if last and i0 < NI:
-                for i in range(i0, i0 + GROUP, 2):
+                for i in range(i0, i0 + group, 2):
                     fold(i)
 
     def row_col():

time: 70.6 us -> 70.6 us (level)
  no operation moved by 1% of the time
where the time goes in v6:
time: 70.6 us; the launch traced here: 70.5 us
  Pallas kernels  69.2 us (98%)
  local copies, waits for them, and re-layouts  1.28 us (2%)
    pallas_call x1, Pallas kernels, normal_equations(): pl.pallas_call(gather_kernel, out_shape=jax.ShapeDtypeStruct((NI, KB), F3...  69.2 us

profile of v6, /device:TPU:32, one launch (start us, length us, event | category | flops | bytes accessed | tf_op | source)
XLA Modules:
  0.0 70.5 jit_solution(14449107055830248426)
XLA Ops:
  0.0 69.2 %normal_equations.1 = f32[8,128]{1,0:T(8,128)} custom-call(bf16[16,128,256]{2,1,0:T(8,128)(2,1)} %bitcast.4, s32[1,8]{1,0:T(1,128)} %bitcast.7, bf16[128,256]{1,0:T(8,128)(2,1)} %item_ref.1, bf16[8,128,128]{2,1,0:T(8,128)(2,1)} %bitcast.5, bf16[8,128,128]{2,1,0:T(8,128)(2,1)} %bitcast.6), custom_call_target="tpu_custom_call" | custom-call | tf_op jit(solution)/shard_map/normal_equations/pallas_call | solution.py:490
  69.2 1.3 %copy.7 = f32[8,128]{1,0:T(8,128)} copy(f32[8,128]{1,0:T(8,128)} %normal_equations.1) | data formatting | bytes 8192
